TPU v7x, 32 devices: a whole 2x2x4 slice. The times are simulated.
32 devices in a mesh: wide: 8 (over z, y), narrow: 4 (over x, core).
Axes of the slice: x: 2, y: 2, z: 4, core: 2. Of those that a mesh axis runs over, the one named last changes fastest.
Arguments:
- patch_feature_matrix: bfloat16 [768, 100, 512], P(('wide', 'narrow')), may hold values from -6 to 6
- occupied_pane_tally: int32 [32], P(('wide', 'narrow')), may hold values from 8 to 24, as said below
- mask_zone_labels: int32 [768, 100], P(('wide', 'narrow')), may hold values from 0 to 8, as said below
- opening_scale_factor: bfloat16 [512], P(('wide', 'narrow')), may hold values from 0.25 to 1.75
- opening_offset: bfloat16 [512], P(('wide', 'narrow')), may hold values from -4 to 4
- qkv_weight_matrix: bfloat16 [512, 1536], P(('wide', 'narrow')), may hold values from -0.375 to 0.375
- question_offset: bfloat16 [512], P(('wide', 'narrow')), may hold values from -4 to 4
- content_offset: bfloat16 [512], P(('wide', 'narrow')), may hold values from -4 to 4
- projection_back_matrix: bfloat16 [512, 512], P(('wide', 'narrow')), may hold values from -1.5 to 1.5
- projection_back_offset: bfloat16 [512], P(('wide', 'narrow')), may hold values from -4 to 4
- central_scale_factor: bfloat16 [512], P(('wide', 'narrow')), may hold values from 0.25 to 1.75
- central_offset: bfloat16 [512], P(('wide', 'narrow')), may hold values from -4 to 4
- widening_matrix: bfloat16 [512, 2048], P(('wide', 'narrow')), may hold values from -0.25 to 0.25
- widening_offset: bfloat16 [2048], P(('wide', 'narrow')), may hold values from -4 to 4
- narrowing_matrix: bfloat16 [2048, 512], P(('wide', 'narrow')), may hold values from -0.1875 to 0.1875
- narrowing_offset: bfloat16 [512], P(('wide', 'narrow')), may hold values from -4 to 4
- displacement_bias_table: bfloat16 [16, 361], replicated, may hold values from -6 to 6
- upstream_sensitivity: bfloat16 [768, 100, 512], P(('wide', 'narrow')), may hold values from -6 to 6
Outputs:
- block_output: bfloat16 [768, 100, 512], P(('wide', 'narrow'))
- grad_input: bfloat16 [768, 100, 512], P(('wide', 'narrow'))
- grad_pregain: float32 [512], P(('wide', 'narrow'))
- opening_offset_derivative: float32 [512], P(('wide', 'narrow'))
- grad_projector: float32 [512, 1536], P(('wide', 'narrow'))
- grad_querybias: float32 [512], P(('wide', 'narrow'))
- grad_valuebias: float32 [512], P(('wide', 'narrow'))
- grad_outmatrix: float32 [512, 512], P(('wide', 'narrow'))
- grad_outbias: float32 [512], P(('wide', 'narrow'))
- grad_midgain: float32 [512], P(('wide', 'narrow'))
- grad_midshift: float32 [512], P(('wide', 'narrow'))
- grad_expander: float32 [512, 2048], P(('wide', 'narrow'))
- grad_expandbias: float32 [2048], P(('wide', 'narrow'))
- grad_reducer: float32 [2048, 512], P(('wide', 'narrow'))
- grad_reducebias: float32 [512], P(('wide', 'narrow'))
- grad_reltable: float32 [16, 361], replicated
Inputs may be any that keep to these rules, and one draw needn't show every extreme that they name: Device d's first occupied_pane_tally[d] slots are live and its other slots are empty; some device has all 24 slots live and some device the fewest. `mask_zone_labels`: inside a window the id is 3 a + b, where a is 0 in windows of no last row and otherwise 1 for window rows below 5 and 2 for the rest, and b likewise over columns.
All inputs are finite; a program needn't handle non-finite values.
Results may differ from a plain program's by a relative error of at most 0.023.
Values may be sent and summed in bfloat16 or wider, within the bound.
No kernel may reach another device: no remote copies, remote signals or barrier semaphores. Data moves between devices by JAX's collectives and lax.ppermute only.
A program may use at most 256 MiB of HBM per device.

v0:
```python
import functools

import jax
import jax.numpy as jnp
from jax import lax
from jax.experimental import pallas as pl
from jax.experimental.pallas import tpu as pltpu
from jax.sharding import PartitionSpec as P

F32 = jnp.float32
BF = jnp.bfloat16
WS = 10
TP = 104
SEG = 128
BLK = 16
EPS = 1e-5
NW = 4
VMEM = 60 << 20

NT = (((1,), (1,)), ((), ()))
TN = (((0,), (0,)), ((), ()))
NN = (((1,), (0,)), ((), ()))


def dot(a, b, dims=NN):
    return lax.dot_general(a, b, dims, preferred_element_type=F32)


def normalize(v):
    c = v - jnp.mean(v, axis=-1, keepdims=True)
    inv = lax.rsqrt(jnp.mean(c * c, axis=-1, keepdims=True) + EPS)
    return c * inv, inv


def norm_back(g, xhat, inv, gain):
    s = g * gain
    return inv * (
        s
        - jnp.mean(s, axis=-1, keepdims=True)
        - xhat * jnp.mean(s * xhat, axis=-1, keepdims=True)
    )


def head_masks():
    lane = lax.broadcasted_iota(jnp.int32, (1, 128), 1)
    return [(lane // 32) == h for h in range(4)]


def head_ones():
    return [jnp.where(m, 1.0, 0.0).astype(BF) for m in head_masks()]


def stack_heads(v, ones):
    return jnp.concatenate([v * m for m in ones], axis=0)


def load_rows(src_ref):
    return src_ref[...].astype(F32).reshape(NW * TP, src_ref.shape[2])


def fetch_blocks(me, sources, parts, sem):
    copies = []
    for s, src in enumerate(sources):
        for z in range(src.shape[0]):
            m = 8 * z + 2 * (s % 4) + s // 4
            d = m ^ me
            for k, (row, rows, dst, lanes) in enumerate(parts):
                to = pl.ds(pl.multiple_of(d * rows, rows), rows)
                copies.append(
                    pltpu.make_async_copy(
                        src.at[z, pl.ds(row, rows), :], dst.at[to, lanes], sem.at[k, m]
                    )
                )
    for c in copies:
        c.start()
    for c in copies:
        c.wait()


def split_blocks(bit, keep_ref, send_ref, row, rows, acc, cols=None):
    lanes = slice(None) if cols is None else cols
    for k in range(acc.shape[0] // (2 * rows)):
        mine = pl.multiple_of(k * 2 * rows + bit * rows, rows)
        other = pl.multiple_of(k * 2 * rows + (1 - bit) * rows, rows)
        keep_ref[k, row : row + rows, :] = acc[pl.ds(mine, rows), lanes].astype(BF)
        send_ref[k, row : row + rows, :] = acc[pl.ds(other, rows), lanes].astype(BF)


def block_at(i, scal):
    return jnp.minimum(i, (scal[0] + NW - 1) // NW - 1)


def whole(shape):
    return pl.BlockSpec(shape, lambda *a: (0,) * len(shape))


def rows_spec(cols, col=0):
    return pl.BlockSpec((NW * TP, cols), lambda i, scal, *r: (block_at(i, scal), col))


def win_spec(shape, live_only=True):
    if live_only:
        return pl.BlockSpec(
            (NW,) + shape, lambda i, scal, *r: (block_at(i, scal),) + (0,) * len(shape)
        )
    return pl.BlockSpec((NW,) + shape, lambda i, *r: (i,) + (0,) * len(shape))


def any_spec():
    return pl.BlockSpec(memory_space=pl.ANY)


def call(body, name, grid, prefetch, args, in_specs, out_shape, out_specs, scratch, cost, gate=()):
    first = len(prefetch) + len(args)

    def without_gate(*refs):
        body(*refs[:first], *refs[first + len(gate) :])

    return pl.pallas_call(
        without_gate,
        grid_spec=pltpu.PrefetchScalarGridSpec(
            num_scalar_prefetch=len(prefetch),
            grid=grid,
            in_specs=list(in_specs) + [any_spec()] * len(gate),
            out_specs=out_specs,
            scratch_shapes=scratch,
        ),
        out_shape=out_shape,
        compiler_params=pltpu.CompilerParams(vmem_limit_bytes=VMEM),
        cost_estimate=pl.CostEstimate(
            flops=int(cost * 8e8), bytes_accessed=int(cost * 1e6), transcendentals=0
        ),
        name=name,
    )(*prefetch, *args, *gate)


def sds(shape, dtype):
    return jax.ShapeDtypeStruct(shape, dtype)


def attention_body(
    scal, x_ref, reg_ref, bias_ref, *refs
):
    sources, refs = refs[:8], refs[8:]
    first_ref, qkv_ref, p_ref, ctx_ref, prm_ref, bw_ref, js, cs, wq, sem = refs
    i = pl.program_id(0)
    width = x_ref.shape[2]
    rows = NW * TP
    live = scal[0]

    @pl.when(i == 0)
    def _():
        js[rows : rows + SEG - TP, :] = jnp.zeros((SEG - TP, 3 * width), F32)
        fetch_blocks(scal[1], sources, [(0, BLK, wq, slice(None))], sem)
        small = wq[:, 3 * width :].astype(F32)
        shares = jnp.concatenate([small[r : r + 1] for r in range(0, width, BLK)], axis=0)
        count = width // BLK
        place = lax.broadcasted_iota(jnp.int32, (count, width), 1)
        mine = place // BLK == lax.broadcasted_iota(jnp.int32, (count, width), 0)
        source = lax.broadcasted_iota(jnp.int32, (128, width), 0)
        target = lax.broadcasted_iota(jnp.int32, (128, width), 1) % BLK
        for v in range(8):
            pick = jnp.where(source == target + BLK * v, 1.0, 0.0).astype(BF)
            spread = dot(shares.astype(BF), pick)
            prm_ref[v : v + 1, :] = jnp.sum(jnp.where(mine, spread, 0.0), axis=0, keepdims=True)
        left = lax.broadcasted_iota(jnp.int32, (1, 128), 1) < 64
        for k in range(width // (2 * BLK)):
            r = 2 * BLK * k
            right = pltpu.roll(small[r + BLK : r + BLK + 8], 64, 1)[1:2]
            bw_ref[0:1, 128 * k : 128 * k + 128] = jnp.where(left, small[r + 1 : r + 2], right)

    @pl.when(i * NW < live)
    def _():
        xhat, _ = normalize(load_rows(x_ref))
        first = (xhat * prm_ref[0:1, :] + prm_ref[1:2, :]).astype(BF)
        first_ref[...] = first
        scale = 32.0**-0.5
        for part in range(3):
            j = dot(first, wq[:, part * width : (part + 1) * width])
            if part == 0:
                j = (j + prm_ref[2:3, :]) * scale
            if part == 2:
                j = j + prm_ref[3:4, :]
            js[0:rows, part * width : (part + 1) * width] = j
        ones = head_ones()
        eye = lax.broadcasted_iota(jnp.int32, (TP, SEG), 0) == lax.broadcasted_iota(
            jnp.int32, (TP, SEG), 1
        )
        masks = []
        for w in range(NW):
            qkv_ref[w] = js[w * TP : w * TP + SEG, :].astype(BF)
            row = jnp.broadcast_to(reg_ref[w], (TP, SEG))
            col = jnp.max(jnp.where(eye, row, -1.0), axis=1, keepdims=True)
            masks.append(jnp.where(row == col, 0.0, -1e30))

        def scores(n):
            w, g = n
            c = 128 * g
            keys = stack_heads(qkv_ref[w, :, width + c : width + c + 128], ones)
            return dot(qkv_ref[w, 0:TP, c : c + 128], keys, NT)

        def softmax(n, s):
            w, g = n
            out = []
            for h in range(4):
                lanes = slice(SEG * h, SEG * (h + 1))
                sh = s[:, lanes] + bias_ref[g, :, lanes] + masks[w]
                e = jnp.exp(sh - jnp.max(sh, axis=1, keepdims=True))
                out.append((e * (1.0 / jnp.sum(e, axis=1, keepdims=True))).astype(BF))
            p = jnp.concatenate(out, axis=1)
            p_ref[w, g] = p
            return p

        def values(n, p):
            w, g = n
            c = 128 * g
            stacked = stack_heads(qkv_ref[w, :, 2 * width + c : 2 * width + c + 128], ones)
            cs[w * TP : (w + 1) * TP, c : c + 128] = dot(p, stacked)

        pairs = [(w, g) for w in range(NW) for g in range(width // 128)]
        for k in range(0, len(pairs), 8):
            part = pairs[k : k + 8]
            ss = [scores(n) for n in part]
            pp = [softmax(n, s) for n, s in zip(part, ss)]
            for n, p in zip(part, pp):
                values(n, p)
        ctx_ref[...] = cs[...].astype(BF)


def attention_forward(scal, x, regions, bias, sources, gate):
    windows, _, width = x.shape
    rows = NW * TP
    groups = width // 128
    return call(
        attention_body, "attn_fwd", (windows // NW,), (scal,), [x, regions, bias] + sources,
        [win_spec((TP, width)), win_spec((1, SEG)), whole(bias.shape)] + [any_spec()] * 8,
        [sds((windows * TP, width), BF), sds((windows, SEG, 3 * width), BF),
         sds((windows, groups, TP, 512), BF), sds((windows * TP, width), BF),
         sds((8, width), F32), sds((1, 4 * width), F32)],
        [rows_spec(width), win_spec((SEG, 3 * width)), win_spec((groups, TP, 512)), rows_spec(width),
         whole((8, width)), whole((1, 4 * width))],
        [pltpu.VMEM((rows + SEG - TP, 3 * width), F32),
         pltpu.VMEM((rows, width), F32), pltpu.VMEM((width, sources[0].shape[2]), BF),
         pltpu.SemaphoreType.DMA((1, width // BLK))],
        24, gate,
    )


def normal_parts(z):
    return 0.5 + 0.5 * lax.erf(z * 0.7071067811865476), jnp.exp(z * z * -0.5)


def hidden_body(
    tokens, scal, x_ref, u_ref, ctx_ref, prm_ref, bw_ref, *refs
):
    sources, refs = refs[:8], refs[8:]
    out_ref, gr_ref, gc_ref, eb_ref, sb_ref, keep_ref, send_ref = refs[:7]
    acts, gps, er, rr, om, wo, wn, ww, sem = refs[7:]
    i = pl.program_id(0)
    width = x_ref.shape[2]
    hidden = ww.shape[1]
    live = scal[0]
    step = 256

    @pl.when(i == 0)
    def _():
        parts = [(0, BLK, wo, slice(None)), (BLK, 4 * BLK, wn, slice(None))]
        for c in range(4):
            parts.append(((5 + c) * BLK, BLK, ww, slice(c * width, (c + 1) * width)))
        fetch_blocks(scal[1], sources, parts, sem)
        er[...] = jnp.zeros_like(er)
        rr[...] = jnp.zeros_like(rr)
        om[...] = jnp.zeros_like(om)
        eb_ref[...] = jnp.zeros_like(eb_ref)
        sb_ref[...] = jnp.zeros_like(sb_ref)

    @pl.when(i * NW >= live)
    def _():
        out_ref[...] = x_ref[:, 0:tokens, :]

    @pl.when(i * NW < live)
    def _():
        xs = load_rows(x_ref)
        row = lax.broadcasted_iota(jnp.int32, (NW * TP, 1), 0)
        us = jnp.where(row < (live - i * NW) * TP, load_rows(u_ref), 0.0)
        ctx = ctx_ref[...]
        up = us.astype(BF)
        res = xs + dot(ctx, wo[...]) + prm_ref[4:5, :]
        xhat, inv = normalize(res)
        second = (xhat * prm_ref[5:6, :] + prm_ref[6:7, :]).astype(BF)

        def products(c):
            cols = slice(c * step, (c + 1) * step)
            return dot(up, wn[cols, :], NT), dot(second, ww[:, cols])

        def activate(c, ga, z):
            cols = slice(c * step, (c + 1) * step)
            z = z + bw_ref[:, cols]
            phi, bell = normal_parts(z)
            acts[:, cols] = (z * phi).astype(BF)
            gp = (ga * (phi + z * bell * 0.3989422804014327)).astype(BF)
            gps[:, cols] = gp
            eb_ref[:, cols] += jnp.sum(gp.astype(F32), axis=0, keepdims=True)

        count = hidden // step
        t = products(0)
        for c in range(count):
            later = products(c + 1) if c + 1 < count else None
            activate(c, *t)
            t = later
        gs = dot(gps[...], ww[...], NT)
        o = res + dot(acts[...], wn[...]) + prm_ref[7:8, :]
        for w in range(NW):
            out_ref[w] = jnp.where(
                i * NW + w < live, o[w * TP : w * TP + tokens], xs[w * TP : w * TP + tokens]
            ).astype(BF)
        gres = us + norm_back(gs, xhat, inv, prm_ref[5:6, :])
        gr_ref[...] = gres
        ga = gres.astype(BF)
        for c in range(count):
            cols = slice(c * step, (c + 1) * step)
            er[:, cols] += dot(second, gps[:, cols], TN)
            rr[cols, :] += dot(acts[:, cols], up, TN)
        om[...] += dot(ctx, ga, TN)
        sb_ref[0:1, :] += jnp.sum(us, axis=0, keepdims=True)
        sb_ref[1:2, :] += jnp.sum(ga.astype(F32), axis=0, keepdims=True)
        gc = dot(ga, wo[...], NT)
        for w in range(NW):
            gc_ref[w] = gc[w * TP : (w + 1) * TP].astype(BF)

    @pl.when(i == pl.num_programs(0) - 1)
    def _():
        bit = scal[1] & 1
        split_blocks(bit, keep_ref, send_ref, 0, BLK, om)
        split_blocks(bit, keep_ref, send_ref, BLK, 4 * BLK, rr)
        for c in range(4):
            split_blocks(
                bit, keep_ref, send_ref, (5 + c) * BLK, BLK, er, slice(c * width, (c + 1) * width)
            )


def hidden_both(scal, tokens, x, u, ctx, prm, bw, sources):
    windows, _, width = x.shape
    hidden = 4 * width
    rows = NW * TP
    pairs = width // BLK // 2
    share = (pairs, 9 * BLK, width)
    return call(
        functools.partial(hidden_body, tokens), "hidden", (windows // NW,), (scal,),
        [x, u, ctx, prm, bw] + sources,
        [win_spec((TP, width), False), win_spec((TP, width)), rows_spec(width),
         whole(prm.shape), whole(bw.shape)] + [any_spec()] * 8,
        [sds((windows, tokens, width), BF), sds((windows * TP, width), F32), sds((windows, TP, width), BF),
         sds((1, hidden), F32), sds((2, width), F32), sds(share, BF), sds(share, BF)],
        [win_spec((tokens, width), False), rows_spec(width), win_spec((TP, width)),
         whole((1, hidden)), whole((2, width)), whole(share), whole(share)],
        [pltpu.VMEM((rows, hidden), BF), pltpu.VMEM((rows, hidden), BF),
         pltpu.VMEM((width, hidden), F32), pltpu.VMEM((hidden, width), F32), pltpu.VMEM((width, width), F32),
         pltpu.VMEM((width, width), BF), pltpu.VMEM((hidden, width), BF), pltpu.VMEM((width, hidden), BF),
         pltpu.SemaphoreType.DMA((6, 2 * pairs))],
        52,
    )


def three_terms(v):
    hi = v.astype(BF)
    rest = v - hi.astype(F32)
    mid = rest.astype(BF)
    return hi, mid, (rest - mid.astype(F32)).astype(BF)


def table_row(scores):
    side = 2 * WS - 1
    reach = side * (WS - 1) + WS - 1
    j = lax.broadcasted_iota(jnp.int32, (SEG, 256), 0)
    k = lax.broadcasted_iota(jnp.int32, (SEG, 256), 1)
    pick = jnp.where(k == reach - (side * (j // WS) + j % WS), 1.0, 0.0).astype(BF)
    u = sum(dot(t, pick) for t in three_terms(scores))
    u = jnp.concatenate([u, jnp.zeros((TP, 128), F32)], axis=1)
    u = pltpu.roll(u, 0, 1, stride=1, stride_axis=0)
    r = lax.broadcasted_iota(jnp.int32, (16, TP), 0)
    i = lax.broadcasted_iota(jnp.int32, (16, TP), 1)
    group = jnp.where(r == i // WS, 1.0, 0.0).astype(BF)
    v = sum(dot(group, t) for t in three_terms(u))
    skip = side - WS
    low = pltpu.roll(v[0:8], 0, 1, stride=skip, stride_axis=0)
    high = pltpu.roll(v[8:16], 0, 1, stride=skip, stride_axis=0)
    return jnp.sum(low + pltpu.roll(high, 8 * skip, 1), axis=0, keepdims=True)


def attention_back_body(
    scal, qkv_ref, p_ref, gc_ref, first_ref, eb_ref, sb_ref,
    gj_ref, keep_ref, send_ref,
    gjs, pj, gb, ra, small,
):
    i = pl.program_id(0)
    width = gc_ref.shape[2]
    live = scal[0]

    @pl.when(i == 0)
    def _():
        pj[...] = jnp.zeros_like(pj)
        gb[...] = jnp.zeros_like(gb)
        ra[...] = jnp.zeros_like(ra)
        small[...] = jnp.zeros_like(small)

    @pl.when(i * NW < live)
    def _():
        masks = head_masks()
        ones = head_ones()
        scale = 32.0**-0.5

        def lanes_of(g, part=0):
            c = part * width + 128 * g
            return slice(c, c + 128)

        def to_probs(n):
            w, g = n
            stacked = stack_heads(qkv_ref[w, :, lanes_of(g, 2)], ones)
            return dot(gc_ref[w, :, lanes_of(g)], stacked, NT)

        def softmax_back(n, dp):
            w, g = n
            out = []
            for h in range(4):
                lanes = slice(SEG * h, SEG * (h + 1))
                ph = p_ref[w, g, :, lanes].astype(F32)
                t = dp[:, lanes] * ph
                out.append(t - ph * jnp.sum(t, axis=1, keepdims=True))
            return jnp.concatenate(out, axis=1).astype(BF)

        def combine(r):
            o = jnp.where(masks[0], r[0:TP], 0.0)
            for h in range(1, 4):
                o = jnp.where(masks[h], r[SEG * h : SEG * h + TP], o)
            return o

        def to_joint(n, ds):
            w, g = n
            rows = slice(w * TP, (w + 1) * TP)
            keys = stack_heads(qkv_ref[w, :, lanes_of(g, 1)], ones)
            gjs[rows, lanes_of(g)] = dot(ds, keys) * scale
            gjs[rows, lanes_of(g, 1)] = combine(dot(ds, qkv_ref[w, 0:TP, lanes_of(g)], TN))
            gjs[rows, lanes_of(g, 2)] = combine(dot(p_ref[w, g], gc_ref[w, :, lanes_of(g)], TN))

        pairs = [(w, g) for g in range(width // 128) for w in range(NW)]
        size = 2
        parts = [pairs[k : k + size] for k in range(0, len(pairs), size)]
        dps = [to_probs(n) for n in parts[0]]
        before = None
        for k, group in enumerate(parts):
            later = [to_probs(n) for n in parts[k + 1]] if k + 1 < len(parts) else None
            dss = [softmax_back(n, dp) for n, dp in zip(group, dps)]
            if before is not None:
                for n, ds in zip(*before):
                    to_joint(n, ds)
            total = dss[0].astype(F32)
            for ds in dss[1:]:
                total += ds.astype(F32)
            ra[group[0][1]] += total
            before = (group, dss)
            dps = later
        for n, ds in zip(*before):
            to_joint(n, ds)
        gj = gjs[...].astype(BF)
        gj_ref[...] = gj
        gb[...] += jnp.sum(gj.astype(F32), axis=0, keepdims=True)
        pj[...] += dot(first_ref[...], gj, TN)

    @pl.when(i == pl.num_programs(0) - 1)
    def _():
        split_blocks(scal[1] & 1, keep_ref, send_ref, 0, BLK, pj)
        for h in range(width // 32):
            lanes = slice(SEG * (h % 4), SEG * (h % 4 + 1))
            small[h : h + 1, 0:384] = table_row(ra[h // 4, :, lanes])
        small[0:1, 384:1408] = eb_ref[:, 0:1024]
        small[1:2, 384:1408] = eb_ref[:, 1024:2048]
        small[2:3, 384:896] = sb_ref[0:1, :]
        small[2:3, 896:1408] = sb_ref[1:2, :]
        small[3:4, 384:1408] = gb[:, 0:1024]
        small[4:5, 384:896] = gb[:, 1024:1536]
        sums = small[...].astype(BF)
        keep_ref[keep_ref.shape[0] - 1] = sums
        send_ref[send_ref.shape[0] - 1] = sums


def read_small(v):
    table = v[:, 0:384]
    eb = jnp.concatenate([v[0:1, 384:1408], v[1:2, 384:1408]], axis=1)
    gb = jnp.concatenate([v[3:4, 384:1408], v[4:5, 384:896]], axis=1)
    return table, eb, v[2:3, 384:896], v[2:3, 896:1408], gb


def attention_back(scal, qkv, p, gc, first, eb, sb, gate):
    windows = qkv.shape[0]
    width = gc.shape[2]
    rows = NW * TP
    groups = width // 128
    share = (width // BLK // 2 + 1, BLK, 3 * width)
    return call(
        attention_back_body, "attn_back", (windows // NW,), (scal,),
        (qkv, p, gc, first, eb, sb),
        [win_spec((SEG, 3 * width)), win_spec((groups, TP, 512)), win_spec((TP, width)),
         rows_spec(width), whole(eb.shape), whole(sb.shape)],
        [sds((windows * TP, 3 * width), BF), sds(share, BF), sds(share, BF)],
        [rows_spec(3 * width), whole(share), whole(share)],
        [pltpu.VMEM((rows, 3 * width), F32), pltpu.VMEM((width, 3 * width), F32),
         pltpu.VMEM((1, 3 * width), F32), pltpu.VMEM((groups, TP, 512), F32),
         pltpu.VMEM((16, 3 * width), F32)],
        27, gate,
    )


def input_grad_body(tokens, scal, x_ref, u_ref, gj_ref, gr_ref, prm_ref, *refs):
    sources = refs[:8]
    gi_ref, wq, sem = refs[8:]
    i = pl.program_id(0)
    width = x_ref.shape[2]
    live = scal[0]

    @pl.when(i == 0)
    def _():
        fetch_blocks(scal[1], sources, [(0, BLK, wq, slice(None))], sem)

    @pl.when(i * NW >= live)
    def _():
        gi_ref[...] = u_ref[:, 0:tokens, :]

    @pl.when(i * NW < live)
    def _():
        us = load_rows(u_ref)
        xhat, inv = normalize(load_rows(x_ref))
        gf = dot(gj_ref[...], wq[:, 0 : 3 * width], NT)
        o = gr_ref[...] + norm_back(gf, xhat, inv, prm_ref[0:1, :])
        for w in range(NW):
            rows = slice(w * TP, w * TP + tokens)
            gi_ref[w] = jnp.where(i * NW + w < live, o[rows], us[rows]).astype(BF)


def input_grad(scal, tokens, x, u, gj, gr, prm, sources, gate):
    windows, _, width = x.shape
    return call(
        functools.partial(input_grad_body, tokens), "input_grad", (windows // NW,), (scal,),
        [x, u, gj, gr, prm] + sources,
        [win_spec((TP, width)), win_spec((TP, width), False), rows_spec(3 * width),
         rows_spec(width), whole(prm.shape)] + [any_spec()] * 8,
        [sds((windows, tokens, width), BF)],
        [win_spec((tokens, width), False)],
        [pltpu.VMEM((width, sources[0].shape[2]), BF), pltpu.SemaphoreType.DMA((1, width // BLK))],
        12, gate,
    )[0]


AXES = ("wide", "narrow")


def exchange(v, mask, n):
    return lax.ppermute(v, AXES, [(i, i ^ mask) for i in range(n)])


def join_body(scal, *refs):
    out = refs[-1]
    size = refs[0].shape[0]
    for k, r in enumerate(refs[:-1]):
        out[k * size : (k + 1) * size] = r[...]


def join(scal, arrays, gate):
    shape = (arrays[0].shape[0] * len(arrays),) + arrays[0].shape[1:]
    return call(
        join_body, "join", (), (scal,), arrays, [whole(a.shape) for a in arrays],
        [sds(shape, BF)], [whole(shape)], [], 0.01, gate,
    )[0]


def hand_on(scal, arrays, gate):
    count = len(arrays)
    return pl.pallas_call(
        lambda *refs: None,
        grid_spec=pltpu.PrefetchScalarGridSpec(
            num_scalar_prefetch=1,
            grid=(),
            in_specs=[any_spec()] * (count + len(gate)),
            out_specs=[any_spec()] * count,
        ),
        out_shape=[sds(a.shape, a.dtype) for a in arrays],
        input_output_aliases={1 + k: k for k in range(count)},
        name="hand_on",
    )(scal, *arrays, *gate)


def pack_joint_body(scal, wqkv_ref, *refs):
    vectors, out = refs[:-1], refs[-1]
    width = wqkv_ref.shape[1]
    out[0, :, 0:width] = wqkv_ref[...]

    def row(ref, at):
        v = ref[...].astype(F32).reshape(1, ref.shape[0])
        rest = 128 - ref.shape[0] - at
        parts = [jnp.zeros((1, at), F32)] * (at > 0) + [v] + [jnp.zeros((1, rest), F32)] * (rest > 0)
        return jnp.concatenate(parts, axis=1)

    first = sum(row(r, BLK * k) for k, r in enumerate(vectors[:8]))
    small = jnp.concatenate([first, row(vectors[8], 0), jnp.zeros((BLK - 2, 128), F32)], axis=0)
    out[0, :, width:] = small.astype(BF)


def pack_joint(scal, wqkv, vectors):
    rows, width = wqkv.shape
    shape = (1, rows, width + 128)
    args = [wqkv] + vectors
    return call(
        pack_joint_body, "pack_joint", (), (scal,), args, [whole(a.shape) for a in args],
        [sds(shape, BF)], [whole(shape)], [], 0.01,
    )[0]


def pack_hidden_body(scal, wout_ref, narrow_ref, widen_ref, out):
    width = wout_ref.shape[1]
    out[0, 0:BLK] = wout_ref[...]
    out[0, BLK : 5 * BLK] = narrow_ref[...]
    for c in range(4):
        out[0, (5 + c) * BLK : (6 + c) * BLK] = widen_ref[:, c * width : (c + 1) * width]


def pack_hidden(scal, wout, narrow, widen, gate):
    shape = (1, 9 * BLK, wout.shape[1])
    args = [wout, narrow, widen]
    return call(
        pack_hidden_body, "pack_hidden", (), (scal,), args, [whole(a.shape) for a in args],
        [sds(shape, BF)], [whole(shape)], [], 0.01, gate,
    )[0]


def others(v, shift, n):
    return [exchange(v, m << shift, n) for m in (1, 2, 3)]


def total_at(ins, at):
    total = ins[0][at].astype(F32)
    for r in ins[1:]:
        total += r[at].astype(F32)
    return total


def deal_body(count, shift, extra, scal, *refs):
    ins, outs = refs[:count], refs[-4:]
    me = (scal[1] >> shift) & 3
    quads = ins[0].shape[0] // 4
    for q in range(quads):
        for m in range(4):
            outs[m][q] = total_at(ins, 4 * q + (m ^ me)).astype(BF)
    if extra:
        rest = total_at(ins, 4 * quads).astype(BF)
        for m in range(4):
            outs[m][quads] = rest


def deal(scal, arrays, shift, gate):
    blocks, rows, cols = arrays[0].shape
    quads, extra = blocks // 4, blocks % 4
    count = len(arrays)
    if extra or quads == 1:
        grid, spec_in, spec_out = (), whole(arrays[0].shape), whole((quads + extra, rows, cols))
    else:
        grid = (quads,)
        spec_in = pl.BlockSpec((4, rows, cols), lambda i, s: (i, 0, 0))
        spec_out = pl.BlockSpec((1, rows, cols), lambda i, s: (i, 0, 0))
    return call(
        functools.partial(deal_body, count, shift, extra), "deal", grid, (scal,),
        arrays, [spec_in] * count,
        [sds((quads + extra, rows, cols), BF)] * 4, [spec_out] * 4, [], 0.01, gate,
    )


def finish_hidden_body(scal, a, b, c, d, expander_ref, outmatrix_ref, reducer_ref):
    v = total_at([a, b, c, d], 0)
    width = v.shape[1]
    outmatrix_ref[...] = v[0:BLK]
    reducer_ref[...] = v[BLK : 5 * BLK]
    for k in range(4):
        expander_ref[:, k * width : (k + 1) * width] = v[(5 + k) * BLK : (6 + k) * BLK]


def finish_hidden(scal, arrays, gate):
    width = arrays[0].shape[2]
    shapes = [(BLK, 4 * width), (BLK, width), (4 * BLK, width)]
    return call(
        finish_hidden_body, "finish_hidden", (), (scal,), arrays,
        [whole(a.shape) for a in arrays],
        [sds(s, F32) for s in shapes], [whole(s) for s in shapes], [], 0.01, gate,
    )


def finish_joint_body(
    scal, a, b, c, d, wqkv_ref, widen_ref, expander_ref, small_ref,
    projector_ref, table_ref, pregain_ref, shift_ref, qb_ref, vb_ref, ob_ref, midgain_ref,
    midshift_ref, xb_ref, rb_ref,
):
    me = scal[1]
    ins = [a, b, c, d]
    projector = total_at(ins, 0)
    width = projector.shape[1] // 3
    projector_ref[...] = projector
    table, eb, reducebias, outbias, gb = read_small(total_at(ins, 1))
    table_ref[...] = table[:, 0 : table_ref.shape[1]]

    shares = small_ref[0][:, small_ref.shape[2] - 128 :].astype(F32)
    eye = lax.broadcasted_iota(jnp.int32, (BLK, 128), 0)
    lanes = lax.broadcasted_iota(jnp.int32, (BLK, 128), 1)

    def column(k):
        return jnp.sum(jnp.where(lanes == eye + BLK * k, shares[0:1], 0.0), axis=1, keepdims=True)

    def gains(w_ref, grad, bias, shift, gain):
        w = w_ref[...].astype(F32)
        g = jnp.sum(w * (grad - shift * bias), axis=1, keepdims=True) / gain
        return g, jnp.sum(w * bias, axis=1, keepdims=True)

    pregain, offset = gains(wqkv_ref, projector, gb, column(1), column(0))
    midgain, midshift = gains(widen_ref, expander_ref[...], eb, column(6), column(5))
    lane = lax.broadcasted_iota(jnp.int32, (BLK, 128), 1)
    mat = jnp.where(lane == 0, pregain, 0.0)
    for k, v in ((1, offset), (2, midgain), (3, midshift)):
        mat = jnp.where(lane == k, v, mat)
    mat = jnp.transpose(mat)
    for k, r in enumerate((pregain_ref, shift_ref, midgain_ref, midshift_ref)):
        r[...] = mat[k : k + 1, 0:BLK]

    def mine(v, size):
        lanes = v.shape[1]
        v = pltpu.roll(jnp.broadcast_to(v, (8, lanes)), lanes - me * size, 1)
        return v[0:1, 0:size]

    qb_ref[...] = mine(gb[:, 0:width], BLK)
    vb_ref[...] = mine(gb[:, 2 * width : 3 * width], BLK)
    ob_ref[...] = mine(outbias, BLK)
    rb_ref[...] = mine(reducebias, BLK)
    xb_ref[...] = mine(eb, 4 * BLK)


def finish_joint(scal, arrays, wqkv, widen, expander, small, entries):
    args = list(arrays) + [wqkv, widen, expander, small]
    row = (1, BLK)
    shapes = [wqkv.shape, (BLK, entries)] + [row] * 7 + [(1, 4 * BLK), row]
    return call(
        finish_joint_body, "finish_joint", (), (scal,), args, [whole(a.shape) for a in args],
        [sds(s, F32) for s in shapes], [whole(s) for s in shapes], [], 0.01,
    )


def score_bias(table, tokens):
    heads = table.shape[0]
    position = jnp.arange(WS * WS, dtype=jnp.int32)
    r, c = position // WS, position % WS
    offset = (
        (r[:, None] - r[None, :] + WS - 1) * (2 * WS - 1) + c[:, None] - c[None, :] + WS - 1
    )
    entries = jnp.arange((2 * WS - 1) ** 2, dtype=jnp.int32)
    onehot = (offset.reshape(-1, 1) == entries[None, :]).astype(BF)
    bias = lax.dot_general(table, onehot, NT, preferred_element_type=F32)
    bias = bias.reshape(heads // 4, 4, tokens, tokens).transpose(0, 2, 1, 3)
    bias = jnp.pad(bias, ((0, 0), (0, TP - tokens), (0, 0), (0, SEG - tokens)))
    return bias.reshape(heads // 4, TP, 4 * SEG)


def as_sources(v):
    return [v[2 * q + c :: 8] for c in (0, 1) for q in range(4)]


def per_device(
    x, tally, labels, gain1, shift1, wqkv, qbias, vbias, wout, obias,
    gain2, shift2, widen, widen_b, narrow, narrow_b, table, up,
):
    tokens, width = x.shape[1:]
    heads, entries = table.shape
    n = lax.axis_size("wide") * lax.axis_size("narrow")
    me = lax.axis_index("wide") * lax.axis_size("narrow") + lax.axis_index("narrow")
    me = me.astype(jnp.int32)
    own = width // n
    fast = own == BLK and n == 32
    scal = jnp.stack([tally[0], me if fast else jnp.int32(0)])
    blocks = width // BLK

    vectors = [gain1, shift1, qbias, vbias, obias, gain2, shift2, narrow_b]
    bias = score_bias(table, tokens)
    x = jnp.pad(x, ((0, 0), (0, TP - tokens), (0, 0)))
    up = jnp.pad(up, ((0, 0), (0, TP - tokens), (0, 0)))
    regions = jnp.pad(labels.astype(F32), ((0, 0), (0, SEG - tokens)), constant_values=-1.0)
    regions = regions[:, None, :]

    if fast:
        pay_q = pack_joint(scal, wqkv, vectors + [widen_b])
        near_q = join(scal, [pay_q] + others(pay_q, 3, n), [])
        pay_a = pack_hidden(scal, wout, narrow, widen, [pay_q])
        sources_q = [near_q] + others(near_q, 1, n)
        sources_q += [exchange(v, 1, n) for v in sources_q]
        near_a = join(scal, [pay_a] + others(pay_a, 3, n), [x, up, bias, regions] + sources_q[1:4])
        got_a = others(near_a, 1, n)
        start = [near_a]
    else:
        def gather(v):
            return lax.all_gather(v, AXES, axis=0, tiled=True)

        def blocked(v, rows):
            return gather(v).reshape(blocks, rows, -1)

        shares = jnp.stack([gather(v).reshape(blocks, BLK) for v in vectors], axis=1)
        rows = jnp.stack(
            [shares.reshape(blocks, 128), jnp.pad(blocked(widen_b, 64)[:, :, 0], ((0, 0), (0, 64)))], axis=1
        )
        every = jnp.pad(rows, ((0, 0), (0, BLK - 2), (0, 0)))
        sources_q = as_sources(jnp.concatenate([blocked(wqkv, BLK), every], axis=2))
        wide = blocked(widen, BLK).reshape(blocks, BLK, 4, width).transpose(0, 2, 1, 3)
        sources_a = as_sources(
            jnp.concatenate(
                [blocked(wout, BLK), blocked(narrow, 4 * BLK), wide.reshape(blocks, 4 * BLK, width)], axis=1
            )
        )
        start = []

    first, qkv, p, ctx, prm, bw = attention_forward(scal, x, regions, bias, sources_q, start)
    if fast:
        sources_a = list(hand_on(scal, [near_a] + got_a, [ctx]))
        sources_a += [exchange(v, 1, n) for v in sources_a]
    out, gr, gc, eb, sb, keep_h, send_h = hidden_both(scal, tokens, x, up, ctx, prm, bw, sources_a)
    between, last = [], []
    if fast:
        dealt_h = deal(scal, [keep_h, exchange(send_h, 1, n)], 1, [])
        got_h = others_of(dealt_h, 1, n)
        between = [dealt_h[0]]
    gj, keep_j, send_j = attention_back(scal, qkv, p, gc, first, eb, sb, between)
    if fast:
        dealt_h = deal(scal, [dealt_h[0]] + got_h, 3, [keep_j])
        got_h = others_of(dealt_h, 3, n)
        (send_j,) = hand_on(scal, [send_j], [dealt_h[0]])
        dealt_j = deal(scal, [keep_j, exchange(send_j, 1, n)], 1, [])
        got_j = others_of(dealt_j, 1, n)
        last = [dealt_h[0], dealt_j[0]]
    grad_in = input_grad(scal, tokens, x, up, gj, gr, prm, sources_q, last)
    if fast:
        dealt_j = deal(scal, [dealt_j[0]] + got_j, 3, [grad_in] + got_h)
        got_j = others_of(dealt_j, 3, n)
        expander, outmatrix, reducer = finish_hidden(scal, [dealt_h[0]] + got_h, [dealt_j[0]])
        done = finish_joint(scal, [dealt_j[0]] + got_j, wqkv, widen, expander, pay_q, entries)
        projector, grad_table = done[:2]
        pregain, offset, qb, vb, ob, midgain, midshift, xb, rb = [v.reshape(-1) for v in done[2:]]
    else:
        def scatter(v):
            return lax.psum_scatter(v, AXES, scatter_dimension=0, tiled=True).astype(F32)

        def natural(keep, send):
            pairs = blocks // 2
            return jnp.stack([keep[:pairs], send[:pairs]], axis=1).reshape((blocks,) + keep.shape[1:])

        all_h = natural(keep_h, send_h)
        outmatrix = scatter(all_h[:, :BLK].reshape(width, width))
        reducer = scatter(all_h[:, BLK : 5 * BLK].reshape(4 * width, width))
        expander = all_h[:, 5 * BLK :].reshape(blocks, 4, BLK, width).transpose(0, 2, 1, 3)
        expander = scatter(expander.reshape(width, 4 * width))
        projector = scatter(natural(keep_j, send_j).reshape(width, 3 * width))
        sums = lax.psum(keep_j[-1].astype(F32), AXES)
        grad_table, eb, rb, ob, gb = read_small(sums)
        grad_table = grad_table[:, :entries]

        def gains(w, grad, bias, shift, gain):
            w = w.astype(F32)
            g = jnp.sum(w * (grad - shift.astype(F32)[:, None] * bias), axis=1)
            return g / gain.astype(F32), jnp.sum(w * bias, axis=1)

        pregain, offset = gains(wqkv, projector, gb, shift1, gain1)
        midgain, midshift = gains(widen, expander, eb, shift2, gain2)

        def mine(v, size):
            return lax.dynamic_slice_in_dim(v[0], me * size, size, 0)

        qb, vb = mine(gb[:, :width], own), mine(gb[:, 2 * width :], own)
        ob, rb, xb = mine(ob, own), mine(rb, own), mine(eb, 4 * own)
    return (
        out, grad_in, pregain, offset, projector, qb, vb, outmatrix, ob, midgain, midshift,
        expander, xb, reducer, rb, grad_table,
    )


def others_of(dealt, shift, n):
    return [exchange(dealt[m], m << shift, n) for m in (1, 2, 3)]


def solution(mesh):
    both = ("wide", "narrow")
    v1, v2, v3 = P(both), P(both, None), P(both, None, None)
    in_specs = (v3, v1, v2, v1, v1, v2, v1, v1, v2, v1, v1, v1, v2, v1, v2, v1, P(), v3)
    out_specs = (v3, v3, v1, v1, v2, v1, v1, v2, v1, v1, v1, v2, v1, v2, v1, P())
    return jax.shard_map(
        per_device, mesh=mesh, in_specs=in_specs, out_specs=out_specs, check_vma=False
    )
```

profile of v0, /device:TPU:0, one launch (start us, length us, event | category | flops | bytes accessed | tf_op | source)
XLA Modules:
  0.0 234.6 jit_solution(6172050120655352219)
XLA Ops:
  2.0 2.2 pack_joint.1.refs_1_.refs_4_.refs_8_
  4.2 5.0 %collective-permute-start.2 = (bf16[1,16,1664]{2,1,0:T(8,128)(2,1)}, bf16[1,16,1664]{2,1,0:T(8,128)(2,1)S(1)}, u32[]{:S(2)}, u32[]{:S(2)}) collective-permute-start(bf16[1,16,1664]{2,1,0:T(8,128)(2,1)} %pack_joint.1.refs_1_.refs_4_.refs_8_), channel_id=1, source_target_pairs={{0,24},{1,25},{2,26},{3,27},{4,28},{5,29},{6,30},{7,31},{8,16},{9,... | collective-permute-start | bytes 159752 | tf_op jit(solution)/shard_map/ppermute | solution.py:558
  12.1 3.8 %collective-permute-start.12 = (bf16[1,144,512]{2,1,0:T(8,128)(2,1)}, bf16[1,144,512]{2,1,0:T(8,128)(2,1)S(1)}, u32[]{:S(2)}, u32[]{:S(2)}) collective-permute-start(bf16[1,144,512]{2,1,0:T(8,128)(2,1)} %pack_hidden.1.refs_1_), channel_id=1, source_target_pairs={{0,24},{1,25},{2,26},{3,27},{4,28},{5,29},{6,30},{7,31},{8,16},{9,... | collective-permute-start | bytes 442376 | tf_op jit(solution)/shard_map/ppermute | solution.py:558
  17.9 2.3 join.2.refs_4_.refs_6_
  20.1 2.4 %collective-permute-start.5 = (bf16[4,16,1664]{2,1,0:T(8,128)(2,1)}, bf16[4,16,1664]{2,1,0:T(8,128)(2,1)S(1)}, u32[]{:S(2)}, u32[]{:S(2)}) collective-permute-start(bf16[4,16,1664]{2,1,0:T(8,128)(2,1)} %join.2.refs_4_.refs_6_), channel_id=1, source_target_pairs={{0,6},{1,7},{2,4},{3,5},{4,2},{5,3},{6,0},{7,1},{8,14},{9,15},{10,... | collective-permute-start | bytes 638984 | tf_op jit(solution)/shard_map/ppermute | solution.py:558
  23.9 2.3 collective-permute-start.10
  29.2 2.6 %collective-permute-done.4.refs_10_.refs_6_.refs_8_ = bf16[4,16,1664]{2,1,0:T(8,128)(2,1)} collective-permute-done((bf16[4,16,1664]{2,1,0:T(8,128)(2,1)}, bf16[4,16,1664]{2,1,0:T(8,128)(2,1)}, u32[]{:S(2)}, u32[]{:S(2)}) %collective-permute-start.4) | collective-permute-done | bytes 213024 | tf_op jit(solution)/shard_map/ppermute | solution.py:558
  32.4 2.9 %fusion.1 = f32[16,10000]{1,0:T(8,128)S(1)} fusion(bf16[16,361]{1,0:T(8,128)(2,1)S(1)} %copy-done, s32[10000]{0:T(1024)S(1)} %reshape.153), kind=kOutput, calls=%fused_computation.2 | convolution fusion | flops 119130000 | bytes 691552 | tf_op jit(solution)/shard_map/dot_general | solution.py:761
  43.9 2.7 %join.3.refs_12_.refs_1_ = bf16[4,144,512]{2,1,0:T(8,128)(2,1)} custom-call(s32[2]{0:T(128)} %pad_add_fusion.refs_0_, bf16[1,144,512]{2,1,0:T(8,128)(2,1)} %pack_hidden.1.refs_1_, bf16[1,144,512]{2,1,0:T(8,128)(2,1)} %collective-permute-done.10.refs_2_, bf16[1,144,512]{2,1,0:T(8,128)(2,1)} %copy-done.22, bf16[1,144,512]{2,1,0:T(8,128)(2,1)} %copy-done.21, ...), custom_call_target="tpu_custom_call" | custom-call | flops 8000000 | bytes 10000 | tf_op jit(solution)/shard_map/join/pallas_call | solution.py:119
  50.0 26.1 %attn_fwd.1 = (bf16[2496,512]{1,0:T(8,128)(2,1)}, bf16[24,128,1536]{2,1,0:T(8,128)(2,1)}, bf16[24,4,104,512]{3,2,1,0:T(8,128)(2,1)}, bf16[2496,512]{1,0:T(8,128)...) custom-call(s32[2]{0:T(128)} %pad_add_fusion.refs_0_, bf16[24,104,512]{2,1,0:T(8,128)(2,1)} %pad.15.refs_5_.refs_1_, ...), custom_call_target="tpu_custom_call" | custom-call | flops 19200000000 | bytes 24000000 | tf_op jit(solution)/shard_map/attn_fwd/pallas_call | solution.py:119
  83.7 55.3 %hidden.1 = (bf16[24,100,512]{2,1,0:T(8,128)(2,1)}, f32[2496,512]{1,0:T(8,128)}, bf16[24,104,512]{2,1,0:T(8,128)(2,1)}, f32[1,2048]{1,0:T(1,128)}, f32[2,512]{1,...) custom-call(s32[2]{0:T(128)} %pad_add_fusion.refs_0_, ...), custom_call_target="tpu_custom_call" | custom-call | flops 41600000000 | bytes 52000000 | tf_op jit(solution)/shard_map/hidden/pallas_call | solution.py:119
  139.1 4.7 %collective-permute-done.20.refs_2_ = bf16[16,144,512]{2,1,0:T(8,128)(2,1)S(1)} collective-permute-done((bf16[16,144,512]{2,1,0:T(8,128)(2,1)}, bf16[16,144,512]{2,1,0:T(8,128)(2,1)S(1)}, u32[]{:S(2)}, u32[]{:S(2)}) %collective-permute-start.20) | collective-permute-done | bytes 2359328 | tf_op jit(solution)/shard_map/ppermute | solution.py:558
  145.2 5.0 %deal.4 = (bf16[4,144,512]{2,1,0:T(8,128)(2,1)}, bf16[4,144,512]{2,1,0:T(8,128)(2,1)}, bf16[4,144,512]{2,1,0:T(8,128)(2,1)}, bf16[4,144,512]{2,1,0:T(8,128)(2,1)}) custom-call(s32[2]{0:T(128)} %pad_add_fusion.refs_0_, bf16[16,144,512]{2,1,0:T(8,128)(2,1)} %get-tuple-element.80.refs_1_, bf16[16,144,512]{2,1,0:T(8,128)(2,1)} %copy-done.6), custom_call_target="tpu_custom_call" | custom-call | flops 8000000 | bytes 10000 | tf_op jit(solution)/shard_map/deal/pallas_call | solution.py:119
  150.3 2.3 collective-permute-start.22
  153.8 30.3 %attn_back.1 = (bf16[2496,1536]{1,0:T(8,128)(2,1)}, bf16[17,16,1536]{2,1,0:T(8,128)(2,1)}, bf16[17,16,1536]{2,1,0:T(8,128)(2,1)}) custom-call(s32[2]{0:T(128)} %pad_add_fusion.refs_0_, bf16[24,128,1536]{2,1,0:T(8,128)(2,1)} %get-tuple-element.74.refs_1_, bf16[24,4,104,512]{3,2,1,0:T(8,128)(2,1)} %get-tuple-element.75.refs_2_, ...), custom_call_target="tpu_custom_call" | custom-call | flops 21600000000 | bytes 27000000 | tf_op jit(solution)/shard_map/attn_back/pallas_call | solution.py:119
  185.3 3.3 %deal.5 = (bf16[1,144,512]{2,1,0:T(8,128)(2,1)}, bf16[1,144,512]{2,1,0:T(8,128)(2,1)}, bf16[1,144,512]{2,1,0:T(8,128)(2,1)}, bf16[1,144,512]{2,1,0:T(8,128)(2,1)}) custom-call(s32[2]{0:T(128)} %pad_add_fusion.refs_0_, bf16[4,144,512]{2,1,0:T(8,128)(2,1)} %get-tuple-element.82.refs_7_.refs_1_, bf16[4,144,512]{2,1,0:T(8,128)(2,1)} %copy-done.14, ...), custom_call_target="tpu_custom_call" | custom-call | flops 8000000 | bytes 10000 | tf_op jit(solution)/shard_map/deal/pallas_call | solution.py:119
  191.5 2.4 %collective-permute-start.30 = (bf16[1,144,512]{2,1,0:T(8,128)(2,1)}, bf16[1,144,512]{2,1,0:T(8,128)(2,1)S(1)}, u32[]{:S(2)}, u32[]{:S(2)}) collective-permute-start(bf16[1,144,512]{2,1,0:T(8,128)(2,1)} %get-tuple-element.97), channel_id=1, source_target_pairs={{0,24},{1,25},{2,26},{3,27},{4,28},{5,29},{6,30},{7,31},{8,16},{9,... | collective-permute-start | bytes 442376 | tf_op jit(solution)/shard_map/ppermute | solution.py:558
  194.7 3.1 %deal.6 = (bf16[5,16,1536]{2,1,0:T(8,128)(2,1)}, bf16[5,16,1536]{2,1,0:T(8,128)(2,1)}, bf16[5,16,1536]{2,1,0:T(8,128)(2,1)}, bf16[5,16,1536]{2,1,0:T(8,128)(2,1)}) custom-call(s32[2]{0:T(128)} %pad_add_fusion.refs_0_, bf16[17,16,1536]{2,1,0:T(8,128)(2,1)} %get-tuple-element.88.refs_5_.refs_1_, bf16[17,16,1536]{2,1,0:T(8,128)(2,1)} %copy-done.7), custom_call_target="tpu_custom_call" | custom-call | flops 8000000 | bytes 10000 | tf_op jit(solution)/shard_map/deal/pallas_call | solution.py:119
  201.4 13.9 %input_grad.1.refs_5_ = bf16[24,100,512]{2,1,0:T(8,128)(2,1)} custom-call(s32[2]{0:T(128)} %pad_add_fusion.refs_0_, bf16[24,104,512]{2,1,0:T(8,128)(2,1)} %pad.15.refs_5_.refs_1_, bf16[24,104,512]{2,1,0:T(8,128)(2,1)} %pad.16.refs_6_.refs_2_, bf16[2496,1536]{1,0:T(8,128)(2,1)} %get-tuple-element.83.refs_3_, f32[2496,512]{1,0:T(8,128)} %get-tuple-element.84.refs_4_, ...), custom_call_target="tpu_custom_call" | custom-call | flops 9600000000 | bytes 12000000 | tf_op jit(solution)/shard_map/input_grad/pallas_call | solution.py:119
  216.8 2.8 %deal.7 = (bf16[2,16,1536]{2,1,0:T(8,128)(2,1)}, bf16[2,16,1536]{2,1,0:T(8,128)(2,1)}, bf16[2,16,1536]{2,1,0:T(8,128)(2,1)}, bf16[2,16,1536]{2,1,0:T(8,128)(2,1)}) custom-call(s32[2]{0:T(128)} %pad_add_fusion.refs_0_, bf16[5,16,1536]{2,1,0:T(8,128)(2,1)} %get-tuple-element.91.refs_15_.refs_1_, bf16[5,16,1536]{2,1,0:T(8,128)(2,1)} %copy-done.17, ...), custom_call_target="tpu_custom_call" | custom-call | flops 8000000 | bytes 10000 | tf_op jit(solution)/shard_map/deal/pallas_call | solution.py:119
  224.0 2.3 copy.47
  226.3 2.3 copy.48
  228.5 2.5 %finish_hidden.1 = (f32[16,2048]{1,0:T(8,128)}, f32[16,512]{1,0:T(8,128)}, f32[64,512]{1,0:T(8,128)}) custom-call(s32[2]{0:T(128)} %pad_add_fusion.refs_0_, bf16[1,144,512]{2,1,0:T(8,128)(2,1)} %get-tuple-element.89.refs_2_.refs_14_.refs_1_, bf16[1,144,512]{2,1,0:T(8,128)(2,1)} %copy-done.11, bf16[1,144,512]{2,1,0:T(8,128)(2,1)} %copy-done.12, ...), custom_call_target="tpu_custom_call" | custom-call | flops 8000000 | bytes 10000 | tf_op jit(solution)/shard_map/finish_hidden/pallas_call | solution.py:119
  231.8 2.7 %finish_joint.1 = (f32[16,1536]{1,0:T(8,128)}, f32[16,361]{1,0:T(8,128)}, f32[1,16]{1,0:T(1,128)}, f32[1,16]{1,0:T(1,128)}, f32[1,16]{1,0:T(1,128)}, /*index=5*/...) custom-call(s32[2]{0:T(128)} %pad_add_fusion.refs_0_, ...), custom_call_target="tpu_custom_call" | custom-call | flops 8000000 | bytes 10000 | tf_op jit(solution)/shard_map/finish_joint/pallas_call | solution.py:119
  (143 shorter events, 47.6 us)
Async XLA Ops:
  4.2 12.4 %collective-permute-start.2 = (bf16[1,16,1664]{2,1,0:T(8,128)(2,1)}, bf16[1,16,1664]{2,1,0:T(8,128)(2,1)S(1)}, u32[]{:S(2)}, u32[]{:S(2)}) collective-permute-start(bf16[1,16,1664]{2,1,0:T(8,128)(2,1)} %pack_joint.1.refs_1_.refs_4_.refs_8_), channel_id=1, source_target_pairs={{0,24},{1,25},{2,26},{3,27},{4,28},{5,29},{6,30},{7,31},{8,16},{9,... | collective-permute-start | bytes 159752 | tf_op jit(solution)/shard_map/ppermute | solution.py:558
  12.1 11.8 %collective-permute-start.12 = (bf16[1,144,512]{2,1,0:T(8,128)(2,1)}, bf16[1,144,512]{2,1,0:T(8,128)(2,1)S(1)}, u32[]{:S(2)}, u32[]{:S(2)}) collective-permute-start(bf16[1,144,512]{2,1,0:T(8,128)(2,1)} %pack_hidden.1.refs_1_), channel_id=1, source_target_pairs={{0,24},{1,25},{2,26},{3,27},{4,28},{5,29},{6,30},{7,31},{8,16},{9,... | collective-permute-start | bytes 442376 | tf_op jit(solution)/shard_map/ppermute | solution.py:558
  15.9 11.9 %collective-permute-start.11 = (bf16[1,144,512]{2,1,0:T(8,128)(2,1)}, bf16[1,144,512]{2,1,0:T(8,128)(2,1)S(1)}, u32[]{:S(2)}, u32[]{:S(2)}) collective-permute-start(bf16[1,144,512]{2,1,0:T(8,128)(2,1)} %pack_hidden.1.refs_1_), channel_id=1, source_target_pairs={{0,16},{1,17},{2,18},{3,19},{4,20},{5,21},{6,22},{7,23},{8,24},{9,... | collective-permute-start | bytes 442376 | tf_op jit(solution)/shard_map/ppermute | solution.py:558
  22.6 9.2 %collective-permute-start.4 = (bf16[4,16,1664]{2,1,0:T(8,128)(2,1)}, bf16[4,16,1664]{2,1,0:T(8,128)(2,1)}, u32[]{:S(2)}, u32[]{:S(2)}) collective-permute-start(bf16[4,16,1664]{2,1,0:T(8,128)(2,1)} %join.2.refs_4_.refs_6_), channel_id=1, source_target_pairs={{0,4},{1,5},{2,6},{3,7},{4,0},{5,1},{6,2},{7,3},{8,12},{9,13},{10,... | collective-permute-start | bytes 638984 | tf_op jit(solution)/shard_map/ppermute | solution.py:558
  23.9 20.0 %collective-permute-start.10 = (bf16[1,144,512]{2,1,0:T(8,128)(2,1)}, bf16[1,144,512]{2,1,0:T(8,128)(2,1)}, u32[]{:S(2)}, u32[]{:S(2)}) collective-permute-start(bf16[1,144,512]{2,1,0:T(8,128)(2,1)} %pack_hidden.1.refs_1_), channel_id=1, source_target_pairs={{0,8},{1,9},{2,10},{3,11},{4,12},{5,13},{6,14},{7,15},{8,0},{9,1},... | collective-permute-start | bytes 442376 | tf_op jit(solution)/shard_map/ppermute | solution.py:558
  27.8 20.5 %collective-permute-start.6 = (bf16[4,16,1664]{2,1,0:T(8,128)(2,1)}, bf16[4,16,1664]{2,1,0:T(8,128)(2,1)}, u32[]{:S(2)}, u32[]{:S(2)}) collective-permute-start(bf16[4,16,1664]{2,1,0:T(8,128)(2,1)} %join.2.refs_4_.refs_6_), channel_id=1, source_target_pairs={{0,1},{1,0},{2,3},{3,2},{4,5},{5,4},{6,7},{7,6},{8,9},{9,8},{10,11... | collective-permute-start | bytes 638984 | tf_op jit(solution)/shard_map/ppermute | solution.py:558
  29.2 20.2 %collective-permute-start.9 = (bf16[4,16,1664]{2,1,0:T(8,128)(2,1)S(1)}, bf16[4,16,1664]{2,1,0:T(8,128)(2,1)}, u32[]{:S(2)}, u32[]{:S(2)}) collective-permute-start(bf16[4,16,1664]{2,1,0:T(8,128)(2,1)S(1)} %collective-permute-done.5.refs_11_.refs_7_.refs_9_), channel_id=1, source_target_pairs={{0,1},{1,0},{2,3},{3,2},{4,5},{5,4},{6,7},{7,6},{8,9},{9,8},{10,11... | collective-permute-start | bytes 638984 | tf_op jit(solution)/shard_map/ppermute | solution.py:558
  31.8 18.2 %collective-permute-start.8 = (bf16[4,16,1664]{2,1,0:T(8,128)(2,1)}, bf16[4,16,1664]{2,1,0:T(8,128)(2,1)}, u32[]{:S(2)}, u32[]{:S(2)}) collective-permute-start(bf16[4,16,1664]{2,1,0:T(8,128)(2,1)} %collective-permute-done.4.refs_10_.refs_6_.refs_8_), channel_id=1, source_target_pairs={{0,1},{1,0},{2,3},{3,2},{4,5},{5,4},{6,7},{7,6},{8,9},{9,8},{10,11... | collective-permute-start | bytes 638984 | tf_op jit(solution)/shard_map/ppermute | solution.py:558
  31.9 18.1 %collective-permute-start.7 = (bf16[4,16,1664]{2,1,0:T(8,128)(2,1)}, bf16[4,16,1664]{2,1,0:T(8,128)(2,1)}, u32[]{:S(2)}, u32[]{:S(2)}) collective-permute-start(bf16[4,16,1664]{2,1,0:T(8,128)(2,1)} %collective-permute-done.3.refs_9_.refs_5_.refs_7_), channel_id=1, source_target_pairs={{0,1},{1,0},{2,3},{3,2},{4,5},{5,4},{6,7},{7,6},{8,9},{9,8},{10,11... | collective-permute-start | bytes 638984 | tf_op jit(solution)/shard_map/ppermute | solution.py:558
  46.5 29.6 %collective-permute-start.15 = (bf16[4,144,512]{2,1,0:T(8,128)(2,1)}, bf16[4,144,512]{2,1,0:T(8,128)(2,1)S(1)}, u32[]{:S(2)}, u32[]{:S(2)}) collective-permute-start(bf16[4,144,512]{2,1,0:T(8,128)(2,1)} %join.3.refs_12_.refs_1_), channel_id=1, source_target_pairs={{0,6},{1,7},{2,4},{3,5},{4,2},{5,3},{6,0},{7,1},{8,14},{9,15},{10,... | collective-permute-start | bytes 1769480 | tf_op jit(solution)/shard_map/ppermute | solution.py:558
  48.3 27.9 %collective-permute-start.14 = (bf16[4,144,512]{2,1,0:T(8,128)(2,1)}, bf16[4,144,512]{2,1,0:T(8,128)(2,1)S(1)}, u32[]{:S(2)}, u32[]{:S(2)}) collective-permute-start(bf16[4,144,512]{2,1,0:T(8,128)(2,1)} %join.3.refs_12_.refs_1_), channel_id=1, source_target_pairs={{0,4},{1,5},{2,6},{3,7},{4,0},{5,1},{6,2},{7,3},{8,12},{9,13},{10,... | collective-permute-start | bytes 1769480 | tf_op jit(solution)/shard_map/ppermute | solution.py:558
  49.5 26.7 %collective-permute-start.13 = (bf16[4,144,512]{2,1,0:T(8,128)(2,1)}, bf16[4,144,512]{2,1,0:T(8,128)(2,1)S(1)}, u32[]{:S(2)}, u32[]{:S(2)}) collective-permute-start(bf16[4,144,512]{2,1,0:T(8,128)(2,1)} %join.3.refs_12_.refs_1_), channel_id=1, source_target_pairs={{0,2},{1,3},{2,0},{3,1},{4,6},{5,7},{6,4},{7,5},{8,10},{9,11},{10,... | collective-permute-start | bytes 1769480 | tf_op jit(solution)/shard_map/ppermute | solution.py:558
  150.3 33.8 %collective-permute-start.21 = (bf16[4,144,512]{2,1,0:T(8,128)(2,1)}, bf16[4,144,512]{2,1,0:T(8,128)(2,1)S(1)}, u32[]{:S(2)}, u32[]{:S(2)}) collective-permute-start(bf16[4,144,512]{2,1,0:T(8,128)(2,1)} %get-tuple-element.85), channel_id=1, source_target_pairs={{0,2},{1,3},{2,0},{3,1},{4,6},{5,7},{6,4},{7,5},{8,10},{9,11},{10,... | collective-permute-start | bytes 1769480 | tf_op jit(solution)/shard_map/ppermute | solution.py:558
  150.3 33.8 %collective-permute-start.22 = (bf16[4,144,512]{2,1,0:T(8,128)(2,1)}, bf16[4,144,512]{2,1,0:T(8,128)(2,1)S(1)}, u32[]{:S(2)}, u32[]{:S(2)}) collective-permute-start(bf16[4,144,512]{2,1,0:T(8,128)(2,1)} %get-tuple-element.86), channel_id=1, source_target_pairs={{0,4},{1,5},{2,6},{3,7},{4,0},{5,1},{6,2},{7,3},{8,12},{9,13},{10,... | collective-permute-start | bytes 1769480 | tf_op jit(solution)/shard_map/ppermute | solution.py:558
  152.6 31.5 %collective-permute-start.23 = (bf16[4,144,512]{2,1,0:T(8,128)(2,1)}, bf16[4,144,512]{2,1,0:T(8,128)(2,1)S(1)}, u32[]{:S(2)}, u32[]{:S(2)}) collective-permute-start(bf16[4,144,512]{2,1,0:T(8,128)(2,1)} %get-tuple-element.87), channel_id=1, source_target_pairs={{0,6},{1,7},{2,4},{3,5},{4,2},{5,3},{6,0},{7,1},{8,14},{9,15},{10,... | collective-permute-start | bytes 1769480 | tf_op jit(solution)/shard_map/ppermute | solution.py:558
  189.4 10.8 %collective-permute-start.28 = (bf16[1,144,512]{2,1,0:T(8,128)(2,1)}, bf16[1,144,512]{2,1,0:T(8,128)(2,1)S(1)}, u32[]{:S(2)}, u32[]{:S(2)}) collective-permute-start(bf16[1,144,512]{2,1,0:T(8,128)(2,1)} %get-tuple-element.95), channel_id=1, source_target_pairs={{0,8},{1,9},{2,10},{3,11},{4,12},{5,13},{6,14},{7,15},{8,0},{9,1},... | collective-permute-start | bytes 442376 | tf_op jit(solution)/shard_map/ppermute | solution.py:558
  189.4 25.8 %collective-permute-start.29 = (bf16[1,144,512]{2,1,0:T(8,128)(2,1)}, bf16[1,144,512]{2,1,0:T(8,128)(2,1)S(1)}, u32[]{:S(2)}, u32[]{:S(2)}) collective-permute-start(bf16[1,144,512]{2,1,0:T(8,128)(2,1)} %get-tuple-element.96), channel_id=1, source_target_pairs={{0,16},{1,17},{2,18},{3,19},{4,20},{5,21},{6,22},{7,23},{8,24},{9,... | collective-permute-start | bytes 442376 | tf_op jit(solution)/shard_map/ppermute | solution.py:558
  191.5 23.8 %collective-permute-start.30 = (bf16[1,144,512]{2,1,0:T(8,128)(2,1)}, bf16[1,144,512]{2,1,0:T(8,128)(2,1)S(1)}, u32[]{:S(2)}, u32[]{:S(2)}) collective-permute-start(bf16[1,144,512]{2,1,0:T(8,128)(2,1)} %get-tuple-element.97), channel_id=1, source_target_pairs={{0,24},{1,25},{2,26},{3,27},{4,28},{5,29},{6,30},{7,31},{8,16},{9,... | collective-permute-start | bytes 442376 | tf_op jit(solution)/shard_map/ppermute | solution.py:558
  197.9 17.4 %collective-permute-start.25 = (bf16[5,16,1536]{2,1,0:T(8,128)(2,1)}, bf16[5,16,1536]{2,1,0:T(8,128)(2,1)S(1)}, u32[]{:S(2)}, u32[]{:S(2)}) collective-permute-start(bf16[5,16,1536]{2,1,0:T(8,128)(2,1)} %get-tuple-element.92), channel_id=1, source_target_pairs={{0,2},{1,3},{2,0},{3,1},{4,6},{5,7},{6,4},{7,5},{8,10},{9,11},{10,... | collective-permute-start | bytes 737288 | tf_op jit(solution)/shard_map/ppermute | solution.py:558
  199.1 16.3 %collective-permute-start.26 = (bf16[5,16,1536]{2,1,0:T(8,128)(2,1)}, bf16[5,16,1536]{2,1,0:T(8,128)(2,1)S(1)}, u32[]{:S(2)}, u32[]{:S(2)}) collective-permute-start(bf16[5,16,1536]{2,1,0:T(8,128)(2,1)} %get-tuple-element.93), channel_id=1, source_target_pairs={{0,4},{1,5},{2,6},{3,7},{4,0},{5,1},{6,2},{7,3},{8,12},{9,13},{10,... | collective-permute-start | bytes 737288 | tf_op jit(solution)/shard_map/ppermute | solution.py:558
  200.2 15.2 %collective-permute-start.27 = (bf16[5,16,1536]{2,1,0:T(8,128)(2,1)}, bf16[5,16,1536]{2,1,0:T(8,128)(2,1)S(1)}, u32[]{:S(2)}, u32[]{:S(2)}) collective-permute-start(bf16[5,16,1536]{2,1,0:T(8,128)(2,1)} %get-tuple-element.94), channel_id=1, source_target_pairs={{0,6},{1,7},{2,4},{3,5},{4,2},{5,3},{6,0},{7,1},{8,14},{9,15},{10,... | collective-permute-start | bytes 737288 | tf_op jit(solution)/shard_map/ppermute | solution.py:558
  219.6 11.5 %collective-permute-start.31 = (bf16[2,16,1536]{2,1,0:T(8,128)(2,1)}, bf16[2,16,1536]{2,1,0:T(8,128)(2,1)S(1)}, u32[]{:S(2)}, u32[]{:S(2)}) collective-permute-start(bf16[2,16,1536]{2,1,0:T(8,128)(2,1)} %get-tuple-element.99), channel_id=1, source_target_pairs={{0,8},{1,9},{2,10},{3,11},{4,12},{5,13},{6,14},{7,15},{8,0},{9,1},... | collective-permute-start | bytes 294920 | tf_op jit(solution)/shard_map/ppermute | solution.py:558
  219.6 11.5 %collective-permute-start.32 = (bf16[2,16,1536]{2,1,0:T(8,128)(2,1)}, bf16[2,16,1536]{2,1,0:T(8,128)(2,1)S(1)}, u32[]{:S(2)}, u32[]{:S(2)}) collective-permute-start(bf16[2,16,1536]{2,1,0:T(8,128)(2,1)} %get-tuple-element.100), channel_id=1, source_target_pairs={{0,16},{1,17},{2,18},{3,19},{4,20},{5,21},{6,22},{7,23},{8,24},{9,... | collective-permute-start | bytes 294920 | tf_op jit(solution)/shard_map/ppermute | solution.py:558
  221.8 9.3 %collective-permute-start.33 = (bf16[2,16,1536]{2,1,0:T(8,128)(2,1)}, bf16[2,16,1536]{2,1,0:T(8,128)(2,1)S(1)}, u32[]{:S(2)}, u32[]{:S(2)}) collective-permute-start(bf16[2,16,1536]{2,1,0:T(8,128)(2,1)} %get-tuple-element.101), channel_id=1, source_target_pairs={{0,24},{1,25},{2,26},{3,27},{4,28},{5,29},{6,30},{7,31},{8,16},{9,... | collective-permute-start | bytes 294920 | tf_op jit(solution)/shard_map/ppermute | solution.py:558
  (43 other events, 170.9 us)
where the time goes:
time: 235 us
  Pallas kernels  156 us (66%)
  starting transfers between devices  36.2 us (15%)
  local copies, waits for them, and re-layouts  22.2 us (9%)
  waiting for transfers between devices  14.2 us (6%)
  matrix products  2.88 us (1%)
    pallas_call x14, Pallas kernels, call(): pl.pallas_call(without_gate, grid_spec=pltpu.PrefetchScalarGridSpec(num_s...  154 us
    ppermute x34, starting transfers between devices, exchange(): return lax.ppermute(v, AXES, [(i, i ^ mask) for i in range(n)])  36.2 us
    unnamed x71, local copies, waits for them, and re-layouts  16.3 us
    ppermute x34, waiting for transfers between devices, exchange(): return lax.ppermute(v, AXES, [(i, i ^ mask) for i in range(n)])  14.2 us
  transfers between devices with their start and end apart: 34, of which 9 were waited for; matrix products, arithmetic and copies ran while one was open for 7% of the time, Pallas kernels for 35%

commit v1 on v0

--- a/solution.py
+++ b/solution.py
@@ -106,11 +106,17 @@
     return pl.BlockSpec((NW,) + shape, lambda i, *r: (i,) + (0,) * len(shape))
 
 
+def vmem_spec():
+    return pl.BlockSpec(memory_space=pltpu.VMEM)
+
+
 def any_spec():
     return pl.BlockSpec(memory_space=pl.ANY)
 
 
-def call(body, name, grid, prefetch, args, in_specs, out_shape, out_specs, scratch, cost, gate=()):
+def call(
+    body, name, grid, prefetch, args, in_specs, out_shape, out_specs, scratch, cost, gate=(), vmem=VMEM
+):
     first = len(prefetch) + len(args)
 
     def without_gate(*refs):
@@ -126,12 +132,35 @@
             scratch_shapes=scratch,
         ),
         out_shape=out_shape,
-        compiler_params=pltpu.CompilerParams(vmem_limit_bytes=VMEM),
+        compiler_params=pltpu.CompilerParams(vmem_limit_bytes=vmem),
         cost_estimate=pl.CostEstimate(
             flops=int(cost * 8e8), bytes_accessed=int(cost * 1e6), transcendentals=0
         ),
         name=name,
     )(*prefetch, *args, *gate)
+
+
+def small_call(body, name, scal, args, outs, gate=(), far=(), scratch=(), far_out=False):
+    first = 1 + len(args) + len(far)
+
+    def without_gate(*refs):
+        body(*refs[:first], *refs[first + len(gate) :])
+
+    here = pl.BlockSpec(memory_space=pltpu.VMEM)
+    return pl.pallas_call(
+        without_gate,
+        grid_spec=pltpu.PrefetchScalarGridSpec(
+            num_scalar_prefetch=1,
+            grid=(),
+            in_specs=[here] * len(args) + [whole(a.shape) for a in far] + [any_spec()] * len(gate),
+            out_specs=[whole(s) if far_out else here for s, _ in outs],
+            scratch_shapes=list(scratch),
+        ),
+        out_shape=[sds(s, t) if far_out else pltpu.VMEM(s, t) for s, t in outs],
+        compiler_params=pltpu.CompilerParams(vmem_limit_bytes=VMEM if far else 12 << 20),
+        cost_estimate=pl.CostEstimate(flops=1000, bytes_accessed=1000, transcendentals=0),
+        name=name,
+    )(scal, *[pltpu.with_memory_space_constraint(a, pltpu.VMEM) for a in args], *far, *gate)
 
 
 def sds(shape, dtype):
@@ -189,7 +218,9 @@
         masks = []
         for w in range(NW):
             qkv_ref[w] = js[w * TP : w * TP + SEG, :].astype(BF)
-            row = jnp.broadcast_to(reg_ref[w], (TP, SEG))
+            row = reg_ref[pl.ds(i * NW + w, 1), :].astype(F32)
+            row = jnp.concatenate([row, jnp.full((1, SEG - row.shape[1]), -1.0, F32)], axis=1)
+            row = jnp.broadcast_to(row, (TP, SEG))
             col = jnp.max(jnp.where(eye, row, -1.0), axis=1, keepdims=True)
             masks.append(jnp.where(row == col, 0.0, -1e30))
 
@@ -207,23 +238,24 @@
                 sh = s[:, lanes] + bias_ref[g, :, lanes] + masks[w]
                 e = jnp.exp(sh - jnp.max(sh, axis=1, keepdims=True))
                 out.append((e * (1.0 / jnp.sum(e, axis=1, keepdims=True))).astype(BF))
-            p = jnp.concatenate(out, axis=1)
-            p_ref[w, g] = p
-            return p
-
-        def values(n, p):
+            p_ref[w, g] = jnp.concatenate(out, axis=1)
+
+        def values(n):
             w, g = n
             c = 128 * g
             stacked = stack_heads(qkv_ref[w, :, 2 * width + c : 2 * width + c + 128], ones)
-            cs[w * TP : (w + 1) * TP, c : c + 128] = dot(p, stacked)
+            cs[w * TP : (w + 1) * TP, c : c + 128] = dot(p_ref[w, g], stacked)
 
         pairs = [(w, g) for w in range(NW) for g in range(width // 128)]
-        for k in range(0, len(pairs), 8):
-            part = pairs[k : k + 8]
-            ss = [scores(n) for n in part]
-            pp = [softmax(n, s) for n, s in zip(part, ss)]
-            for n, p in zip(part, pp):
-                values(n, p)
+        lag = 3
+        ss = {}
+        for k in range(len(pairs) + lag + 1):
+            if k < len(pairs):
+                ss[k] = scores(pairs[k])
+            if 0 <= k - 1 - lag < len(pairs):
+                values(pairs[k - 1 - lag])
+            if 0 <= k - lag < len(pairs):
+                softmax(pairs[k - lag], ss.pop(k - lag))
         ctx_ref[...] = cs[...].astype(BF)
 
 
@@ -233,7 +265,7 @@
     groups = width // 128
     return call(
         attention_body, "attn_fwd", (windows // NW,), (scal,), [x, regions, bias] + sources,
-        [win_spec((TP, width)), win_spec((1, SEG)), whole(bias.shape)] + [any_spec()] * 8,
+        [win_spec((TP, width)), whole(regions.shape), whole(bias.shape)] + [any_spec()] * 8,
         [sds((windows * TP, width), BF), sds((windows, SEG, 3 * width), BF),
          sds((windows, groups, TP, 512), BF), sds((windows * TP, width), BF),
          sds((8, width), F32), sds((1, 4 * width), F32)],
@@ -315,8 +347,8 @@
                 i * NW + w < live, o[w * TP : w * TP + tokens], xs[w * TP : w * TP + tokens]
             ).astype(BF)
         gres = us + norm_back(gs, xhat, inv, prm_ref[5:6, :])
-        gr_ref[...] = gres
         ga = gres.astype(BF)
+        gr_ref[...] = ga
         for c in range(count):
             cols = slice(c * step, (c + 1) * step)
             er[:, cols] += dot(second, gps[:, cols], TN)
@@ -350,15 +382,15 @@
         [x, u, ctx, prm, bw] + sources,
         [win_spec((TP, width), False), win_spec((TP, width)), rows_spec(width),
          whole(prm.shape), whole(bw.shape)] + [any_spec()] * 8,
-        [sds((windows, tokens, width), BF), sds((windows * TP, width), F32), sds((windows, TP, width), BF),
-         sds((1, hidden), F32), sds((2, width), F32), sds(share, BF), sds(share, BF)],
+        [sds((windows, tokens, width), BF), sds((windows * TP, width), BF), sds((windows, TP, width), BF),
+         sds((1, hidden), F32), sds((2, width), F32), pltpu.VMEM(share, BF), pltpu.VMEM(share, BF)],
         [win_spec((tokens, width), False), rows_spec(width), win_spec((TP, width)),
-         whole((1, hidden)), whole((2, width)), whole(share), whole(share)],
+         whole((1, hidden)), whole((2, width)), vmem_spec(), vmem_spec()],
         [pltpu.VMEM((rows, hidden), BF), pltpu.VMEM((rows, hidden), BF),
          pltpu.VMEM((width, hidden), F32), pltpu.VMEM((hidden, width), F32), pltpu.VMEM((width, width), F32),
          pltpu.VMEM((width, width), BF), pltpu.VMEM((hidden, width), BF), pltpu.VMEM((width, hidden), BF),
          pltpu.SemaphoreType.DMA((6, 2 * pairs))],
-        52,
+        52, (), 52 << 20,
     )
 
 
@@ -502,12 +534,12 @@
         (qkv, p, gc, first, eb, sb),
         [win_spec((SEG, 3 * width)), win_spec((groups, TP, 512)), win_spec((TP, width)),
          rows_spec(width), whole(eb.shape), whole(sb.shape)],
-        [sds((windows * TP, 3 * width), BF), sds(share, BF), sds(share, BF)],
-        [rows_spec(3 * width), whole(share), whole(share)],
+        [sds((windows * TP, 3 * width), BF), pltpu.VMEM(share, BF), pltpu.VMEM(share, BF)],
+        [rows_spec(3 * width), vmem_spec(), vmem_spec()],
         [pltpu.VMEM((rows, 3 * width), F32), pltpu.VMEM((width, 3 * width), F32),
          pltpu.VMEM((1, 3 * width), F32), pltpu.VMEM((groups, TP, 512), F32),
          pltpu.VMEM((16, 3 * width), F32)],
-        27, gate,
+        27, gate, 56 << 20,
     )
 
 
@@ -531,7 +563,7 @@
         us = load_rows(u_ref)
         xhat, inv = normalize(load_rows(x_ref))
         gf = dot(gj_ref[...], wq[:, 0 : 3 * width], NT)
-        o = gr_ref[...] + norm_back(gf, xhat, inv, prm_ref[0:1, :])
+        o = gr_ref[...].astype(F32) + norm_back(gf, xhat, inv, prm_ref[0:1, :])
         for w in range(NW):
             rows = slice(w * TP, w * TP + tokens)
             gi_ref[w] = jnp.where(i * NW + w < live, o[rows], us[rows]).astype(BF)
@@ -542,8 +574,12 @@
     return call(
         functools.partial(input_grad_body, tokens), "input_grad", (windows // NW,), (scal,),
         [x, u, gj, gr, prm] + sources,
-        [win_spec((TP, width)), win_spec((TP, width), False), rows_spec(3 * width),
-         rows_spec(width), whole(prm.shape)] + [any_spec()] * 8,
+        [win_spec((TP, width)),
+         pl.BlockSpec(
+             (NW, TP, width),
+             lambda i, s: (jnp.maximum(i, jnp.minimum(s[0] // NW, windows // NW - 1)), 0, 0),
+         ),
+         rows_spec(3 * width), rows_spec(width), whole(prm.shape)] + [any_spec()] * 8,
         [sds((windows, tokens, width), BF)],
         [win_spec((tokens, width), False)],
         [pltpu.VMEM((width, sources[0].shape[2]), BF), pltpu.SemaphoreType.DMA((1, width // BLK))],
@@ -567,10 +603,7 @@
 
 def join(scal, arrays, gate):
     shape = (arrays[0].shape[0] * len(arrays),) + arrays[0].shape[1:]
-    return call(
-        join_body, "join", (), (scal,), arrays, [whole(a.shape) for a in arrays],
-        [sds(shape, BF)], [whole(shape)], [], 0.01, gate,
-    )[0]
+    return small_call(join_body, "join", scal, arrays, [(shape, BF)], gate)[0]
 
 
 def hand_on(scal, arrays, gate):
@@ -607,12 +640,8 @@
 
 def pack_joint(scal, wqkv, vectors):
     rows, width = wqkv.shape
-    shape = (1, rows, width + 128)
-    args = [wqkv] + vectors
-    return call(
-        pack_joint_body, "pack_joint", (), (scal,), args, [whole(a.shape) for a in args],
-        [sds(shape, BF)], [whole(shape)], [], 0.01,
-    )[0]
+    outs = [((1, rows, width + 128), BF)]
+    return small_call(pack_joint_body, "pack_joint", scal, [], outs, far=[wqkv] + vectors)[0]
 
 
 def pack_hidden_body(scal, wout_ref, narrow_ref, widen_ref, out):
@@ -626,10 +655,7 @@
 def pack_hidden(scal, wout, narrow, widen, gate):
     shape = (1, 9 * BLK, wout.shape[1])
     args = [wout, narrow, widen]
-    return call(
-        pack_hidden_body, "pack_hidden", (), (scal,), args, [whole(a.shape) for a in args],
-        [sds(shape, BF)], [whole(shape)], [], 0.01, gate,
-    )[0]
+    return small_call(pack_hidden_body, "pack_hidden", scal, [], [(shape, BF)], gate, far=args)[0]
 
 
 def others(v, shift, n):
@@ -659,18 +685,8 @@
 def deal(scal, arrays, shift, gate):
     blocks, rows, cols = arrays[0].shape
     quads, extra = blocks // 4, blocks % 4
-    count = len(arrays)
-    if extra or quads == 1:
-        grid, spec_in, spec_out = (), whole(arrays[0].shape), whole((quads + extra, rows, cols))
-    else:
-        grid = (quads,)
-        spec_in = pl.BlockSpec((4, rows, cols), lambda i, s: (i, 0, 0))
-        spec_out = pl.BlockSpec((1, rows, cols), lambda i, s: (i, 0, 0))
-    return call(
-        functools.partial(deal_body, count, shift, extra), "deal", grid, (scal,),
-        arrays, [spec_in] * count,
-        [sds((quads + extra, rows, cols), BF)] * 4, [spec_out] * 4, [], 0.01, gate,
-    )
+    body = functools.partial(deal_body, len(arrays), shift, extra)
+    return small_call(body, "deal", scal, arrays, [((quads + extra, rows, cols), BF)] * 4, gate)
 
 
 def finish_hidden_body(scal, a, b, c, d, expander_ref, outmatrix_ref, reducer_ref):
@@ -685,10 +701,8 @@
 def finish_hidden(scal, arrays, gate):
     width = arrays[0].shape[2]
     shapes = [(BLK, 4 * width), (BLK, width), (4 * BLK, width)]
-    return call(
-        finish_hidden_body, "finish_hidden", (), (scal,), arrays,
-        [whole(a.shape) for a in arrays],
-        [sds(s, F32) for s in shapes], [whole(s) for s in shapes], [], 0.01, gate,
+    return small_call(
+        finish_hidden_body, "finish_hidden", scal, arrays, [(s, F32) for s in shapes], gate, far_out=True
     )
 
 
@@ -740,28 +754,46 @@
 
 
 def finish_joint(scal, arrays, wqkv, widen, expander, small, entries):
-    args = list(arrays) + [wqkv, widen, expander, small]
     row = (1, BLK)
     shapes = [wqkv.shape, (BLK, entries)] + [row] * 7 + [(1, 4 * BLK), row]
-    return call(
-        finish_joint_body, "finish_joint", (), (scal,), args, [whole(a.shape) for a in args],
-        [sds(s, F32) for s in shapes], [whole(s) for s in shapes], [], 0.01,
+    return small_call(
+        finish_joint_body, "finish_joint", scal, arrays, [(s, F32) for s in shapes],
+        far=[wqkv, widen, expander, small], far_out=True,
     )
 
 
-def score_bias(table, tokens):
+def score_bias_body(scal, table_ref, bias_ref):
+    side = 2 * WS - 1
+    reach = side * (WS - 1) + WS - 1
+    heads, entries = table_ref.shape
+    i = lax.broadcasted_iota(jnp.int32, (TP, 384), 0)
+    e = lax.broadcasted_iota(jnp.int32, (TP, 384), 1)
+    pick = jnp.where(e == reach + side * (i // WS) + i % WS, 1.0, 0.0).astype(BF)
+    j = lax.broadcasted_iota(jnp.int32, (SEG, 16), 0)
+    r = lax.broadcasted_iota(jnp.int32, (SEG, 16), 1)
+    group = jnp.where(r == j // WS, 1.0, 0.0).astype(BF)
+    table = jnp.concatenate(
+        [table_ref[...].astype(F32), jnp.zeros((heads, 384 - entries), F32)], axis=1
+    )
+    skip = side - WS
+    for h in range(heads):
+        t = jnp.broadcast_to(table[h : h + 1], (8, 384))
+        low = pltpu.roll(t, 0, 1, stride=skip, stride_axis=0)
+        v = jnp.concatenate([low, pltpu.roll(low, 8 * skip, 1)], axis=0).astype(BF)
+        u = pltpu.roll(dot(group, v), 0, 1, stride=1, stride_axis=0).astype(BF)
+        bias_ref[h // 4, :, SEG * (h % 4) : SEG * (h % 4 + 1)] = dot(pick, u, NT)
+
+
+def score_bias(scal, table, gate):
     heads = table.shape[0]
-    position = jnp.arange(WS * WS, dtype=jnp.int32)
-    r, c = position // WS, position % WS
-    offset = (
-        (r[:, None] - r[None, :] + WS - 1) * (2 * WS - 1) + c[:, None] - c[None, :] + WS - 1
-    )
-    entries = jnp.arange((2 * WS - 1) ** 2, dtype=jnp.int32)
-    onehot = (offset.reshape(-1, 1) == entries[None, :]).astype(BF)
-    bias = lax.dot_general(table, onehot, NT, preferred_element_type=F32)
-    bias = bias.reshape(heads // 4, 4, tokens, tokens).transpose(0, 2, 1, 3)
-    bias = jnp.pad(bias, ((0, 0), (0, TP - tokens), (0, 0), (0, SEG - tokens)))
-    return bias.reshape(heads // 4, TP, 4 * SEG)
+    shape = (heads // 4, TP, 4 * SEG)
+    return small_call(
+        score_bias_body, "score_bias", scal, [], [(shape, F32)], gate, far=[table], far_out=True
+    )[0]
+
+
+def by_window(v):
+    return jnp.pad(v, ((0, 0), (0, TP - v.shape[1]), (0, 0)))
 
 
 def as_sources(v):
@@ -783,19 +815,16 @@
     blocks = width // BLK
 
     vectors = [gain1, shift1, qbias, vbias, obias, gain2, shift2, narrow_b]
-    bias = score_bias(table, tokens)
-    x = jnp.pad(x, ((0, 0), (0, TP - tokens), (0, 0)))
-    up = jnp.pad(up, ((0, 0), (0, TP - tokens), (0, 0)))
-    regions = jnp.pad(labels.astype(F32), ((0, 0), (0, SEG - tokens)), constant_values=-1.0)
-    regions = regions[:, None, :]
-
     if fast:
         pay_q = pack_joint(scal, wqkv, vectors + [widen_b])
-        near_q = join(scal, [pay_q] + others(pay_q, 3, n), [])
         pay_a = pack_hidden(scal, wout, narrow, widen, [pay_q])
-        sources_q = [near_q] + others(near_q, 1, n)
-        sources_q += [exchange(v, 1, n) for v in sources_q]
-        near_a = join(scal, [pay_a] + others(pay_a, 3, n), [x, up, bias, regions] + sources_q[1:4])
+        x = by_window(x)
+        near_q = join(scal, [pay_q] + others(pay_q, 3, n), [x, pay_a])
+        got_a = others(pay_a, 3, n)
+        bias = score_bias(scal, table, [near_q])
+        sources_q = hand_on(scal, [near_q] + others(near_q, 1, n), [bias] + got_a)
+        near_a = join(scal, [pay_a] + got_a, [sources_q[0]])
+        sources_q = list(sources_q) + [exchange(v, 1, n) for v in sources_q]
         got_a = others(near_a, 1, n)
         start = [near_a]
     else:
@@ -818,11 +847,14 @@
             )
         )
         start = []
-
-    first, qkv, p, ctx, prm, bw = attention_forward(scal, x, regions, bias, sources_q, start)
+        x = by_window(x)
+        bias = score_bias(scal, table, [])
+
+    first, qkv, p, ctx, prm, bw = attention_forward(scal, x, labels, bias, sources_q, start)
     if fast:
         sources_a = list(hand_on(scal, [near_a] + got_a, [ctx]))
         sources_a += [exchange(v, 1, n) for v in sources_a]
+    up = by_window(up)
     out, gr, gc, eb, sb, keep_h, send_h = hidden_both(scal, tokens, x, up, ctx, prm, bw, sources_a)
     between, last = [], []
     if fast:

time: 235 us -> 213 us (0.906)
  Pallas kernels: 156 us -> 125 us
  starting transfers between devices: 36.2 us -> 50.3 us
  matrix products: 2.88 us -> 0 us
    pallas_call x14 -> x4, Pallas kernels: 154 us -> 106 us  [call(): pl.pallas_call(without_gate, grid_spec=pltpu.PrefetchScalarGridSpec(num_s...]
    pallas_call x0 -> x11, Pallas kernels: none -> 16.7 us  [small_call(): pl.pallas_call(without_gate, grid_spec=pltpu.PrefetchScalarGridSpec(num_s...]
    ppermute x34, starting transfers between devices: 36.2 us -> 50.3 us  [exchange(): return lax.ppermute(v, AXES, [(i, i ^ mask) for i in range(n)])]
    unnamed x71 -> x80, local copies, waits for them, and re-layouts: 16.3 us -> 19.9 us
    dot_general x1 -> x0, matrix products: 2.88 us -> none  [score_bias(): bias = lax.dot_general(table, onehot, NT, preferred_element_type=F32)]
  transfers between devices with their start and end apart: 34 -> 34, of which waited for: 9 -> 8; matrix products, arithmetic and copies ran while one was open for 7% -> 5% of each run, Pallas kernels for 35% -> 32%
where the time goes in v1:
time: 213 us; the launch traced here: 212 us
  Pallas kernels  125 us (59%)
  starting transfers between devices  50.3 us (24%)
  local copies, waits for them, and re-layouts  21.7 us (10%)
  waiting for transfers between devices  12.6 us (6%)
    pallas_call x4, Pallas kernels, call(): pl.pallas_call(without_gate, grid_spec=pltpu.PrefetchScalarGridSpec(num_s...  106 us
    ppermute x34, starting transfers between devices, exchange(): return lax.ppermute(v, AXES, [(i, i ^ mask) for i in range(n)])  50.3 us
    unnamed x80, local copies, waits for them, and re-layouts  19.9 us
    pallas_call x11, Pallas kernels, small_call(): pl.pallas_call(without_gate, grid_spec=pltpu.PrefetchScalarGridSpec(num_s...  16.7 us
    ppermute x34, waiting for transfers between devices, exchange(): return lax.ppermute(v, AXES, [(i, i ^ mask) for i in range(n)])  12.6 us
  transfers between devices with their start and end apart: 34, of which 8 were waited for; matrix products, arithmetic and copies ran while one was open for 5% of the time, Pallas kernels for 32%

profile of v1, /device:TPU:0, one launch (start us, length us, event | category | flops | bytes accessed | tf_op | source)
XLA Modules:
  0.0 212.0 jit_solution(8364393447467971381)
XLA Ops:
  5.8 5.1 %collective-permute-start.8 = (bf16[1,144,512]{2,1,0:T(8,128)(2,1)S(1)}, bf16[1,144,512]{2,1,0:T(8,128)(2,1)S(1)}, u32[]{:S(2)}, u32[]{:S(2)}) collective-permute-start(bf16[1,144,512]{2,1,0:T(8,128)(2,1)S(1)} %pack_hidden.1.refs_6_.refs_1_), channel_id=1, source_target_pairs={{0,24},{1,25},{2,26},{3,27},{4,28},{5,29},{6,30},{7,31},{8,16},{9,... | collective-permute-start | bytes 442376 | tf_op jit(solution)/shard_map/ppermute | solution.py:594
  11.9 3.4 %collective-permute-start = (bf16[1,16,1664]{2,1,0:T(8,128)(2,1)}, bf16[1,16,1664]{2,1,0:T(8,128)(2,1)S(1)}, u32[]{:S(2)}, u32[]{:S(2)}) collective-permute-start(bf16[1,16,1664]{2,1,0:T(8,128)(2,1)} %copy-done.6), channel_id=1, source_target_pairs={{0,8},{1,9},{2,10},{3,11},{4,12},{5,13},{6,14},{7,15},{8,0},{9,1},... | collective-permute-start | bytes 159752 | tf_op jit(solution)/shard_map/ppermute | solution.py:594
  15.3 2.5 %copy.43 = bf16[24,100,512]{2,1,0:T(8,128)(2,1)S(1)} copy(bf16[24,100,512]{2,0,1:T(8,128)(2,1)} %param.18) | data formatting | bytes 4915200 | tf_op args[0]
  18.0 3.6 %collective-permute-done.1.refs_3_ = bf16[1,16,1664]{2,1,0:T(8,128)(2,1)S(1)} collective-permute-done((bf16[1,16,1664]{2,1,0:T(8,128)(2,1)}, bf16[1,16,1664]{2,1,0:T(8,128)(2,1)S(1)}, u32[]{:S(2)}, u32[]{:S(2)}) %collective-permute-start.1) | collective-permute-done | bytes 53280 | tf_op jit(solution)/shard_map/ppermute | solution.py:594
  22.2 2.5 %collective-permute-start.5 = (bf16[4,16,1664]{2,1,0:T(8,128)(2,1)S(1)}, bf16[4,16,1664]{2,1,0:T(8,128)(2,1)}, u32[]{:S(2)}, u32[]{:S(2)}) collective-permute-start(bf16[4,16,1664]{2,1,0:T(8,128)(2,1)S(1)} %join.2.refs_2_.refs_1_), channel_id=1, source_target_pairs={{0,6},{1,7},{2,4},{3,5},{4,2},{5,3},{6,0},{7,1},{8,14},{9,15},{10,... | collective-permute-start | bytes 638984 | tf_op jit(solution)/shard_map/ppermute | solution.py:594
  26.8 2.0 collective-permute-start.6
  28.8 5.3 %score_bias.1.refs_5_.refs_3_ = f32[4,104,512]{2,1,0:T(8,128)} custom-call(s32[2]{0:T(128)} %pad_add_fusion.refs_0_, bf16[16,361]{1,0:T(8,128)(2,1)} %refs_1_.5, bf16[4,16,1664]{2,1,0:T(8,128)(2,1)} %copy-done.3), custom_call_target="tpu_custom_call" | custom-call | flops 1000 | bytes 1000 | tf_op jit(solution)/shard_map/score_bias/pallas_call | solution.py:150
  40.8 2.5 %collective-permute-start.15 = (bf16[4,144,512]{2,1,0:T(8,128)(2,1)S(1)}, bf16[4,144,512]{2,1,0:T(8,128)(2,1)S(1)}, u32[]{:S(2)}, u32[]{:S(2)}) collective-permute-start(bf16[4,144,512]{2,1,0:T(8,128)(2,1)S(1)} %join.3.refs_12_.refs_1_), channel_id=1, source_target_pairs={{0,6},{1,7},{2,4},{3,5},{4,2},{5,3},{6,0},{7,1},{8,14},{9,15},{10,... | collective-permute-start | bytes 1769480 | tf_op jit(solution)/shard_map/ppermute | solution.py:594
  45.8 21.9 %attn_fwd.1 = (bf16[2496,512]{1,0:T(8,128)(2,1)}, bf16[24,128,1536]{2,1,0:T(8,128)(2,1)}, bf16[24,4,104,512]{3,2,1,0:T(8,128)(2,1)}, bf16[2496,512]{1,0:T(8,128)...) custom-call(s32[2]{0:T(128)} %pad_add_fusion.refs_0_, bf16[24,104,512]{2,1,0:T(8,128)(2,1)} %copy-done.2, s32[24,100]{1,0:T(8,128)} %refs_2_.5, ...), custom_call_target="tpu_custom_call" | custom-call | flops 19200000000 | bytes 24000000 | tf_op jit(solution)/shard_map/attn_fwd/pallas_call | solution.py:125
  67.8 2.1 collective-permute-done.14.refs_3_
  77.0 46.0 %hidden.1 = (bf16[24,100,512]{2,1,0:T(8,128)(2,1)}, bf16[2496,512]{1,0:T(8,128)(2,1)}, bf16[24,104,512]{2,1,0:T(8,128)(2,1)}, f32[1,2048]{1,0:T(1,128)}, f32[2,5...) custom-call(s32[2]{0:T(128)} %pad_add_fusion.refs_0_, ...), custom_call_target="tpu_custom_call" | custom-call | flops 41600000000 | bytes 52000000 | tf_op jit(solution)/shard_map/hidden/pallas_call | solution.py:125
  123.0 7.8 %collective-permute-start.20 = (bf16[16,144,512]{2,1,0:T(8,128)(2,1)S(1)}, bf16[16,144,512]{2,1,0:T(8,128)(2,1)S(1)}, u32[]{:S(2)}, u32[]{:S(2)}) collective-permute-start(bf16[16,144,512]{2,1,0:T(8,128)(2,1)S(1)} %get-tuple-element.89), channel_id=1, source_target_pairs={{0,1},{1,0},{2,3},{3,2},{4,5},{5,4},{6,7},{7,6},{8,9},{9,8},{10,11... | collective-permute-start | bytes 7077896 | tf_op jit(solution)/shard_map/ppermute | solution.py:594
  130.8 4.2 %collective-permute-done.20.refs_2_ = bf16[16,144,512]{2,1,0:T(8,128)(2,1)S(1)} collective-permute-done((bf16[16,144,512]{2,1,0:T(8,128)(2,1)S(1)}, bf16[16,144,512]{2,1,0:T(8,128)(2,1)S(1)}, u32[]{:S(2)}, u32[]{:S(2)}) %collective-permute-start.20) | collective-permute-done | bytes 2359328 | tf_op jit(solution)/shard_map/ppermute | solution.py:594
  136.9 2.7 %collective-permute-start.22 = (bf16[4,144,512]{2,1,0:T(8,128)(2,1)S(1)}, bf16[4,144,512]{2,1,0:T(8,128)(2,1)S(1)}, u32[]{:S(2)}, u32[]{:S(2)}) collective-permute-start(bf16[4,144,512]{2,1,0:T(8,128)(2,1)S(1)} %get-tuple-element.94), channel_id=1, source_target_pairs={{0,4},{1,5},{2,6},{3,7},{4,0},{5,1},{6,2},{7,3},{8,12},{9,13},{10,... | collective-permute-start | bytes 1769480 | tf_op jit(solution)/shard_map/ppermute | solution.py:594
  141.1 26.1 %attn_back.1 = (bf16[2496,1536]{1,0:T(8,128)(2,1)}, bf16[17,16,1536]{2,1,0:T(8,128)(2,1)S(1)}, bf16[17,16,1536]{2,1,0:T(8,128)(2,1)S(1)}) custom-call(s32[2]{0:T(128)} %pad_add_fusion.refs_0_, bf16[24,128,1536]{2,1,0:T(8,128)(2,1)} %get-tuple-element.82.refs_1_, bf16[24,4,104,512]{3,2,1,0:T(8,128)(2,1)} %get-tuple-element.83.refs_2_, ...), custom_call_target="tpu_custom_call" | custom-call | flops 21600000000 | bytes 27000000 | tf_op jit(solution)/shard_map/attn_back/pallas_call | solution.py:125
  170.3 3.3 %collective-permute-start.24 = (bf16[17,16,1536]{2,1,0:T(8,128)(2,1)}, bf16[17,16,1536]{2,1,0:T(8,128)(2,1)S(1)}, u32[]{:S(2)}, u32[]{:S(2)}) collective-permute-start(bf16[17,16,1536]{2,1,0:T(8,128)(2,1)} %hand_on.5), channel_id=1, source_target_pairs={{0,1},{1,0},{2,3},{3,2},{4,5},{5,4},{6,7},{7,6},{8,9},{9,8},{10,11... | collective-permute-start | bytes 2506760 | tf_op jit(solution)/shard_map/ppermute | solution.py:594
  173.6 3.0 %collective-permute-start.29 = (bf16[1,144,512]{2,1,0:T(8,128)(2,1)S(1)}, bf16[1,144,512]{2,1,0:T(8,128)(2,1)S(1)}, u32[]{:S(2)}, u32[]{:S(2)}) collective-permute-start(bf16[1,144,512]{2,1,0:T(8,128)(2,1)S(1)} %get-tuple-element.104), channel_id=1, source_target_pairs={{0,16},{1,17},{2,18},{3,19},{4,20},{5,21},{6,22},{7,23},{8,24},{9,... | collective-permute-start | bytes 442376 | tf_op jit(solution)/shard_map/ppermute | solution.py:594
  180.0 2.0 collective-permute-start.26
  183.5 12.0 %input_grad.1.refs_5_ = bf16[24,100,512]{2,1,0:T(8,128)(2,1)} custom-call(s32[2]{0:T(128)} %pad_add_fusion.refs_0_, bf16[24,104,512]{2,1,0:T(8,128)(2,1)} %copy-done.2, bf16[24,104,512]{2,1,0:T(8,128)(2,1)} %pad.8.refs_2_, bf16[2496,1536]{1,0:T(8,128)(2,1)} %get-tuple-element.91.refs_3_, bf16[2496,512]{1,0:T(8,128)(2,1)} %get-tuple-element.92.refs_4_, ...), custom_call_target="tpu_custom_call" | custom-call | flops 9600000000 | bytes 12000000 | tf_op jit(solution)/shard_map/input_grad/pallas_call | solution.py:125
  195.5 1.7 copy-done
  198.0 4.1 %collective-permute-start.32 = (bf16[2,16,1536]{2,1,0:T(8,128)(2,1)S(1)}, bf16[2,16,1536]{2,1,0:T(8,128)(2,1)S(1)}, u32[]{:S(2)}, u32[]{:S(2)}) collective-permute-start(bf16[2,16,1536]{2,1,0:T(8,128)(2,1)S(1)} %get-tuple-element.108), channel_id=1, source_target_pairs={{0,16},{1,17},{2,18},{3,19},{4,20},{5,21},{6,22},{7,23},{8,24},{9,... | collective-permute-start | bytes 294920 | tf_op jit(solution)/shard_map/ppermute | solution.py:594
  202.4 2.3 %copy.45 = bf16[24,100,512]{2,0,1:T(8,128)(2,1)} copy(bf16[24,100,512]{2,1,0:T(8,128)(2,1)S(1)} %copy-done.27) | data formatting | bytes 4915200
  204.7 2.3 %copy.46 = bf16[24,100,512]{2,0,1:T(8,128)(2,1)} copy(bf16[24,100,512]{2,1,0:T(8,128)(2,1)S(1)} %copy-done.1) | data formatting | bytes 4915200
  209.3 2.5 %finish_joint.1 = (f32[16,1536]{1,0:T(8,128)}, f32[16,361]{1,0:T(8,128)}, f32[1,16]{1,0:T(1,128)}, f32[1,16]{1,0:T(1,128)}, f32[1,16]{1,0:T(1,128)}, /*index=5*/...) custom-call(s32[2]{0:T(128)} %pad_add_fusion.refs_0_, ...), custom_call_target="tpu_custom_call" | custom-call | flops 1000 | bytes 1000 | tf_op jit(solution)/shard_map/finish_joint/pallas_call | solution.py:150
  (145 shorter events, 39.1 us)
Async XLA Ops:
  5.8 21.0 %collective-permute-start.8 = (bf16[1,144,512]{2,1,0:T(8,128)(2,1)S(1)}, bf16[1,144,512]{2,1,0:T(8,128)(2,1)S(1)}, u32[]{:S(2)}, u32[]{:S(2)}) collective-permute-start(bf16[1,144,512]{2,1,0:T(8,128)(2,1)S(1)} %pack_hidden.1.refs_6_.refs_1_), channel_id=1, source_target_pairs={{0,24},{1,25},{2,26},{3,27},{4,28},{5,29},{6,30},{7,31},{8,16},{9,... | collective-permute-start | bytes 442376 | tf_op jit(solution)/shard_map/ppermute | solution.py:594
  11.0 10.6 %collective-permute-start.1 = (bf16[1,16,1664]{2,1,0:T(8,128)(2,1)}, bf16[1,16,1664]{2,1,0:T(8,128)(2,1)S(1)}, u32[]{:S(2)}, u32[]{:S(2)}) collective-permute-start(bf16[1,16,1664]{2,1,0:T(8,128)(2,1)} %copy-done.6), channel_id=1, source_target_pairs={{0,16},{1,17},{2,18},{3,19},{4,20},{5,21},{6,22},{7,23},{8,24},{9,... | collective-permute-start | bytes 159752 | tf_op jit(solution)/shard_map/ppermute | solution.py:594
  11.9 9.7 %collective-permute-start = (bf16[1,16,1664]{2,1,0:T(8,128)(2,1)}, bf16[1,16,1664]{2,1,0:T(8,128)(2,1)S(1)}, u32[]{:S(2)}, u32[]{:S(2)}) collective-permute-start(bf16[1,16,1664]{2,1,0:T(8,128)(2,1)} %copy-done.6), channel_id=1, source_target_pairs={{0,8},{1,9},{2,10},{3,11},{4,12},{5,13},{6,14},{7,15},{8,0},{9,1},... | collective-permute-start | bytes 159752 | tf_op jit(solution)/shard_map/ppermute | solution.py:594
  22.2 11.9 %collective-permute-start.5 = (bf16[4,16,1664]{2,1,0:T(8,128)(2,1)S(1)}, bf16[4,16,1664]{2,1,0:T(8,128)(2,1)}, u32[]{:S(2)}, u32[]{:S(2)}) collective-permute-start(bf16[4,16,1664]{2,1,0:T(8,128)(2,1)S(1)} %join.2.refs_2_.refs_1_), channel_id=1, source_target_pairs={{0,6},{1,7},{2,4},{3,5},{4,2},{5,3},{6,0},{7,1},{8,14},{9,15},{10,... | collective-permute-start | bytes 638984 | tf_op jit(solution)/shard_map/ppermute | solution.py:594
  24.7 9.4 %collective-permute-start.4 = (bf16[4,16,1664]{2,1,0:T(8,128)(2,1)S(1)}, bf16[4,16,1664]{2,1,0:T(8,128)(2,1)}, u32[]{:S(2)}, u32[]{:S(2)}) collective-permute-start(bf16[4,16,1664]{2,1,0:T(8,128)(2,1)S(1)} %join.2.refs_2_.refs_1_), channel_id=1, source_target_pairs={{0,4},{1,5},{2,6},{3,7},{4,0},{5,1},{6,2},{7,3},{8,12},{9,13},{10,... | collective-permute-start | bytes 638984 | tf_op jit(solution)/shard_map/ppermute | solution.py:594
  25.2 8.9 %collective-permute-start.3 = (bf16[4,16,1664]{2,1,0:T(8,128)(2,1)S(1)}, bf16[4,16,1664]{2,1,0:T(8,128)(2,1)}, u32[]{:S(2)}, u32[]{:S(2)}) collective-permute-start(bf16[4,16,1664]{2,1,0:T(8,128)(2,1)S(1)} %join.2.refs_2_.refs_1_), channel_id=1, source_target_pairs={{0,2},{1,3},{2,0},{3,1},{4,6},{5,7},{6,4},{7,5},{8,10},{9,11},{10,... | collective-permute-start | bytes 638984 | tf_op jit(solution)/shard_map/ppermute | solution.py:594
  25.8 8.3 %collective-permute-start.7 = (bf16[1,144,512]{2,1,0:T(8,128)(2,1)S(1)}, bf16[1,144,512]{2,1,0:T(8,128)(2,1)S(1)}, u32[]{:S(2)}, u32[]{:S(2)}) collective-permute-start(bf16[1,144,512]{2,1,0:T(8,128)(2,1)S(1)} %pack_hidden.1.refs_6_.refs_1_), channel_id=1, source_target_pairs={{0,16},{1,17},{2,18},{3,19},{4,20},{5,21},{6,22},{7,23},{8,24},{9,... | collective-permute-start | bytes 442376 | tf_op jit(solution)/shard_map/ppermute | solution.py:594
  35.6 8.3 %collective-permute-start.11 = (bf16[4,16,1664]{2,1,0:T(8,128)(2,1)}, bf16[4,16,1664]{2,1,0:T(8,128)(2,1)S(1)}, u32[]{:S(2)}, u32[]{:S(2)}) collective-permute-start(bf16[4,16,1664]{2,1,0:T(8,128)(2,1)} %get-tuple-element.72.refs_6_.refs_8_), channel_id=1, source_target_pairs={{0,1},{1,0},{2,3},{3,2},{4,5},{5,4},{6,7},{7,6},{8,9},{9,8},{10,11... | collective-permute-start | bytes 638984 | tf_op jit(solution)/shard_map/ppermute | solution.py:594
  36.0 8.3 %collective-permute-start.12 = (bf16[4,16,1664]{2,1,0:T(8,128)(2,1)}, bf16[4,16,1664]{2,1,0:T(8,128)(2,1)S(1)}, u32[]{:S(2)}, u32[]{:S(2)}) collective-permute-start(bf16[4,16,1664]{2,1,0:T(8,128)(2,1)} %get-tuple-element.73.refs_7_.refs_9_), channel_id=1, source_target_pairs={{0,1},{1,0},{2,3},{3,2},{4,5},{5,4},{6,7},{7,6},{8,9},{9,8},{10,11... | collective-permute-start | bytes 638984 | tf_op jit(solution)/shard_map/ppermute | solution.py:594
  40.8 26.9 %collective-permute-start.15 = (bf16[4,144,512]{2,1,0:T(8,128)(2,1)S(1)}, bf16[4,144,512]{2,1,0:T(8,128)(2,1)S(1)}, u32[]{:S(2)}, u32[]{:S(2)}) collective-permute-start(bf16[4,144,512]{2,1,0:T(8,128)(2,1)S(1)} %join.3.refs_12_.refs_1_), channel_id=1, source_target_pairs={{0,6},{1,7},{2,4},{3,5},{4,2},{5,3},{6,0},{7,1},{8,14},{9,15},{10,... | collective-permute-start | bytes 1769480 | tf_op jit(solution)/shard_map/ppermute | solution.py:594
  43.3 26.5 %collective-permute-start.14 = (bf16[4,144,512]{2,1,0:T(8,128)(2,1)S(1)}, bf16[4,144,512]{2,1,0:T(8,128)(2,1)}, u32[]{:S(2)}, u32[]{:S(2)}) collective-permute-start(bf16[4,144,512]{2,1,0:T(8,128)(2,1)S(1)} %join.3.refs_12_.refs_1_), channel_id=1, source_target_pairs={{0,4},{1,5},{2,6},{3,7},{4,0},{5,1},{6,2},{7,3},{8,12},{9,13},{10,... | collective-permute-start | bytes 1769480 | tf_op jit(solution)/shard_map/ppermute | solution.py:594
  43.9 26.1 %collective-permute-start.13 = (bf16[4,144,512]{2,1,0:T(8,128)(2,1)S(1)}, bf16[4,144,512]{2,1,0:T(8,128)(2,1)}, u32[]{:S(2)}, u32[]{:S(2)}) collective-permute-start(bf16[4,144,512]{2,1,0:T(8,128)(2,1)S(1)} %join.3.refs_12_.refs_1_), channel_id=1, source_target_pairs={{0,2},{1,3},{2,0},{3,1},{4,6},{5,7},{6,4},{7,5},{8,10},{9,11},{10,... | collective-permute-start | bytes 1769480 | tf_op jit(solution)/shard_map/ppermute | solution.py:594
  123.0 12.0 %collective-permute-start.20 = (bf16[16,144,512]{2,1,0:T(8,128)(2,1)S(1)}, bf16[16,144,512]{2,1,0:T(8,128)(2,1)S(1)}, u32[]{:S(2)}, u32[]{:S(2)}) collective-permute-start(bf16[16,144,512]{2,1,0:T(8,128)(2,1)S(1)} %get-tuple-element.89), channel_id=1, source_target_pairs={{0,1},{1,0},{2,3},{3,2},{4,5},{5,4},{6,7},{7,6},{8,9},{9,8},{10,11... | collective-permute-start | bytes 7077896 | tf_op jit(solution)/shard_map/ppermute | solution.py:594
  136.9 31.2 %collective-permute-start.21 = (bf16[4,144,512]{2,1,0:T(8,128)(2,1)S(1)}, bf16[4,144,512]{2,1,0:T(8,128)(2,1)S(1)}, u32[]{:S(2)}, u32[]{:S(2)}) collective-permute-start(bf16[4,144,512]{2,1,0:T(8,128)(2,1)S(1)} %get-tuple-element.93), channel_id=1, source_target_pairs={{0,2},{1,3},{2,0},{3,1},{4,6},{5,7},{6,4},{7,5},{8,10},{9,11},{10,... | collective-permute-start | bytes 1769480 | tf_op jit(solution)/shard_map/ppermute | solution.py:594
  136.9 31.2 %collective-permute-start.22 = (bf16[4,144,512]{2,1,0:T(8,128)(2,1)S(1)}, bf16[4,144,512]{2,1,0:T(8,128)(2,1)S(1)}, u32[]{:S(2)}, u32[]{:S(2)}) collective-permute-start(bf16[4,144,512]{2,1,0:T(8,128)(2,1)S(1)} %get-tuple-element.94), channel_id=1, source_target_pairs={{0,4},{1,5},{2,6},{3,7},{4,0},{5,1},{6,2},{7,3},{8,12},{9,13},{10,... | collective-permute-start | bytes 1769480 | tf_op jit(solution)/shard_map/ppermute | solution.py:594
  139.6 28.5 %collective-permute-start.23 = (bf16[4,144,512]{2,1,0:T(8,128)(2,1)S(1)}, bf16[4,144,512]{2,1,0:T(8,128)(2,1)S(1)}, u32[]{:S(2)}, u32[]{:S(2)}) collective-permute-start(bf16[4,144,512]{2,1,0:T(8,128)(2,1)S(1)} %get-tuple-element.95), channel_id=1, source_target_pairs={{0,6},{1,7},{2,4},{3,5},{4,2},{5,3},{6,0},{7,1},{8,14},{9,15},{10,... | collective-permute-start | bytes 1769480 | tf_op jit(solution)/shard_map/ppermute | solution.py:594
  173.6 8.6 %collective-permute-start.28 = (bf16[1,144,512]{2,1,0:T(8,128)(2,1)S(1)}, bf16[1,144,512]{2,1,0:T(8,128)(2,1)S(1)}, u32[]{:S(2)}, u32[]{:S(2)}) collective-permute-start(bf16[1,144,512]{2,1,0:T(8,128)(2,1)S(1)} %get-tuple-element.103), channel_id=1, source_target_pairs={{0,8},{1,9},{2,10},{3,11},{4,12},{5,13},{6,14},{7,15},{8,0},{9,1},... | collective-permute-start | bytes 442376 | tf_op jit(solution)/shard_map/ppermute | solution.py:594
  173.6 21.8 %collective-permute-start.29 = (bf16[1,144,512]{2,1,0:T(8,128)(2,1)S(1)}, bf16[1,144,512]{2,1,0:T(8,128)(2,1)S(1)}, u32[]{:S(2)}, u32[]{:S(2)}) collective-permute-start(bf16[1,144,512]{2,1,0:T(8,128)(2,1)S(1)} %get-tuple-element.104), channel_id=1, source_target_pairs={{0,16},{1,17},{2,18},{3,19},{4,20},{5,21},{6,22},{7,23},{8,24},{9,... | collective-permute-start | bytes 442376 | tf_op jit(solution)/shard_map/ppermute | solution.py:594
  176.7 18.8 %collective-permute-start.30 = (bf16[1,144,512]{2,1,0:T(8,128)(2,1)S(1)}, bf16[1,144,512]{2,1,0:T(8,128)(2,1)S(1)}, u32[]{:S(2)}, u32[]{:S(2)}) collective-permute-start(bf16[1,144,512]{2,1,0:T(8,128)(2,1)S(1)} %get-tuple-element.105), channel_id=1, source_target_pairs={{0,24},{1,25},{2,26},{3,27},{4,28},{5,29},{6,30},{7,31},{8,16},{9,... | collective-permute-start | bytes 442376 | tf_op jit(solution)/shard_map/ppermute | solution.py:594
  179.5 16.0 %collective-permute-start.25 = (bf16[5,16,1536]{2,1,0:T(8,128)(2,1)S(1)}, bf16[5,16,1536]{2,1,0:T(8,128)(2,1)S(1)}, u32[]{:S(2)}, u32[]{:S(2)}) collective-permute-start(bf16[5,16,1536]{2,1,0:T(8,128)(2,1)S(1)} %get-tuple-element.100), channel_id=1, source_target_pairs={{0,2},{1,3},{2,0},{3,1},{4,6},{5,7},{6,4},{7,5},{8,10},{9,11},{10,... | collective-permute-start | bytes 737288 | tf_op jit(solution)/shard_map/ppermute | solution.py:594
  180.0 15.4 %collective-permute-start.26 = (bf16[5,16,1536]{2,1,0:T(8,128)(2,1)S(1)}, bf16[5,16,1536]{2,1,0:T(8,128)(2,1)S(1)}, u32[]{:S(2)}, u32[]{:S(2)}) collective-permute-start(bf16[5,16,1536]{2,1,0:T(8,128)(2,1)S(1)} %get-tuple-element.101), channel_id=1, source_target_pairs={{0,4},{1,5},{2,6},{3,7},{4,0},{5,1},{6,2},{7,3},{8,12},{9,13},{10,... | collective-permute-start | bytes 737288 | tf_op jit(solution)/shard_map/ppermute | solution.py:594
  182.3 13.2 %collective-permute-start.27 = (bf16[5,16,1536]{2,1,0:T(8,128)(2,1)S(1)}, bf16[5,16,1536]{2,1,0:T(8,128)(2,1)S(1)}, u32[]{:S(2)}, u32[]{:S(2)}) collective-permute-start(bf16[5,16,1536]{2,1,0:T(8,128)(2,1)S(1)} %get-tuple-element.102), channel_id=1, source_target_pairs={{0,6},{1,7},{2,4},{3,5},{4,2},{5,3},{6,0},{7,1},{8,14},{9,15},{10,... | collective-permute-start | bytes 737288 | tf_op jit(solution)/shard_map/ppermute | solution.py:594
  197.9 10.3 %collective-permute-start.31 = (bf16[2,16,1536]{2,1,0:T(8,128)(2,1)S(1)}, bf16[2,16,1536]{2,1,0:T(8,128)(2,1)S(1)}, u32[]{:S(2)}, u32[]{:S(2)}) collective-permute-start(bf16[2,16,1536]{2,1,0:T(8,128)(2,1)S(1)} %get-tuple-element.107), channel_id=1, source_target_pairs={{0,8},{1,9},{2,10},{3,11},{4,12},{5,13},{6,14},{7,15},{8,0},{9,1},... | collective-permute-start | bytes 294920 | tf_op jit(solution)/shard_map/ppermute | solution.py:594
  198.0 11.3 %collective-permute-start.32 = (bf16[2,16,1536]{2,1,0:T(8,128)(2,1)S(1)}, bf16[2,16,1536]{2,1,0:T(8,128)(2,1)S(1)}, u32[]{:S(2)}, u32[]{:S(2)}) collective-permute-start(bf16[2,16,1536]{2,1,0:T(8,128)(2,1)S(1)} %get-tuple-element.108), channel_id=1, source_target_pairs={{0,16},{1,17},{2,18},{3,19},{4,20},{5,21},{6,22},{7,23},{8,24},{9,... | collective-permute-start | bytes 294920 | tf_op jit(solution)/shard_map/ppermute | solution.py:594
  (48 other events, 306.4 us)

commit v2 on v1

--- a/solution.py
+++ b/solution.py
@@ -340,6 +340,10 @@
             later = products(c + 1) if c + 1 < count else None
             activate(c, *t)
             t = later
+        for c in range(count):
+            cols = slice(c * step, (c + 1) * step)
+            er[:, cols] += dot(second, gps[:, cols], TN)
+            rr[cols, :] += dot(acts[:, cols], up, TN)
         gs = dot(gps[...], ww[...], NT)
         o = res + dot(acts[...], wn[...]) + prm_ref[7:8, :]
         for w in range(NW):
@@ -349,10 +353,6 @@
         gres = us + norm_back(gs, xhat, inv, prm_ref[5:6, :])
         ga = gres.astype(BF)
         gr_ref[...] = ga
-        for c in range(count):
-            cols = slice(c * step, (c + 1) * step)
-            er[:, cols] += dot(second, gps[:, cols], TN)
-            rr[cols, :] += dot(acts[:, cols], up, TN)
         om[...] += dot(ctx, ga, TN)
         sb_ref[0:1, :] += jnp.sum(us, axis=0, keepdims=True)
         sb_ref[1:2, :] += jnp.sum(ga.astype(F32), axis=0, keepdims=True)
@@ -776,12 +776,15 @@
         [table_ref[...].astype(F32), jnp.zeros((heads, 384 - entries), F32)], axis=1
     )
     skip = side - WS
+    vs, us = [], []
     for h in range(heads):
         t = jnp.broadcast_to(table[h : h + 1], (8, 384))
         low = pltpu.roll(t, 0, 1, stride=skip, stride_axis=0)
-        v = jnp.concatenate([low, pltpu.roll(low, 8 * skip, 1)], axis=0).astype(BF)
-        u = pltpu.roll(dot(group, v), 0, 1, stride=1, stride_axis=0).astype(BF)
-        bias_ref[h // 4, :, SEG * (h % 4) : SEG * (h % 4 + 1)] = dot(pick, u, NT)
+        vs.append(jnp.concatenate([low, pltpu.roll(low, 8 * skip, 1)], axis=0).astype(BF))
+    for h in range(heads):
+        us.append(pltpu.roll(dot(group, vs[h]), 0, 1, stride=1, stride_axis=0).astype(BF))
+    for h in range(heads):
+        bias_ref[h // 4, :, SEG * (h % 4) : SEG * (h % 4 + 1)] = dot(pick, us[h], NT)
 
 
 def score_bias(scal, table, gate):
@@ -819,10 +822,10 @@
         pay_q = pack_joint(scal, wqkv, vectors + [widen_b])
         pay_a = pack_hidden(scal, wout, narrow, widen, [pay_q])
         x = by_window(x)
-        near_q = join(scal, [pay_q] + others(pay_q, 3, n), [x, pay_a])
+        near_q = join(scal, [pay_q] + others(pay_q, 3, n), [x])
         got_a = others(pay_a, 3, n)
         bias = score_bias(scal, table, [near_q])
-        sources_q = hand_on(scal, [near_q] + others(near_q, 1, n), [bias] + got_a)
+        sources_q = hand_on(scal, [near_q] + others(near_q, 1, n), [bias])
         near_a = join(scal, [pay_a] + got_a, [sources_q[0]])
         sources_q = list(sources_q) + [exchange(v, 1, n) for v in sources_q]
         got_a = others(near_a, 1, n)

time: 213 us -> 210 us (0.986)
  Pallas kernels: 125 us -> 94.9 us
  waiting for transfers between devices: 12.6 us -> 30.4 us
  starting transfers between devices: 50.3 us -> 63.1 us
  local copies, waits for them, and re-layouts: 21.7 us -> 18.1 us
    pallas_call x4, Pallas kernels: 106 us -> 77.5 us  [call(): pl.pallas_call(without_gate, grid_spec=pltpu.PrefetchScalarGridSpec(num_s...]
    ppermute x34, waiting for transfers between devices: 12.6 us -> 30.4 us  [exchange(): return lax.ppermute(v, AXES, [(i, i ^ mask) for i in range(n)])]
    ppermute x34, starting transfers between devices: 50.3 us -> 63.1 us  [exchange(): return lax.ppermute(v, AXES, [(i, i ^ mask) for i in range(n)])]
    unnamed x80 -> x68, local copies, waits for them, and re-layouts: 19.9 us -> 16.3 us
  transfers between devices with their start and end apart: 34 -> 34, of which waited for: 8 -> 12; matrix products, arithmetic and copies ran while one was open for 5% -> 5% of each run, Pallas kernels for 32% -> 26%
where the time goes in v2:
time: 210 us; the launch traced here: 209 us
  Pallas kernels  94.9 us (45%)
  starting transfers between devices  63.1 us (30%)
  waiting for transfers between devices  30.4 us (14%)
  local copies, waits for them, and re-layouts  18.1 us (9%)
    pallas_call x4, Pallas kernels, call(): pl.pallas_call(without_gate, grid_spec=pltpu.PrefetchScalarGridSpec(num_s...  77.5 us
    ppermute x34, starting transfers between devices, exchange(): return lax.ppermute(v, AXES, [(i, i ^ mask) for i in range(n)])  63.1 us
    ppermute x34, waiting for transfers between devices, exchange(): return lax.ppermute(v, AXES, [(i, i ^ mask) for i in range(n)])  30.4 us
    unnamed x68, local copies, waits for them, and re-layouts  16.3 us
    pallas_call x11, Pallas kernels, small_call(): pl.pallas_call(without_gate, grid_spec=pltpu.PrefetchScalarGridSpec(num_s...  15.3 us
  transfers between devices with their start and end apart: 34, of which 12 were waited for; matrix products, arithmetic and copies ran while one was open for 5% of the time, Pallas kernels for 26%

profile of v2, /device:TPU:0, one launch (start us, length us, event | category | flops | bytes accessed | tf_op | source)
XLA Modules:
  0.0 208.9 jit_solution(5471191817393277744)
XLA Ops:
  3.5 5.1 %collective-permute-start.2 = (bf16[1,16,1664]{2,1,0:T(8,128)(2,1)S(1)}, bf16[1,16,1664]{2,1,0:T(8,128)(2,1)S(1)}, u32[]{:S(2)}, u32[]{:S(2)}) collective-permute-start(bf16[1,16,1664]{2,1,0:T(8,128)(2,1)S(1)} %pack_joint.1.refs_1_.refs_4_.refs_8_), channel_id=1, source_target_pairs={{0,24},{1,25},{2,26},{3,27},{4,28},{5,29},{6,30},{7,31},{8,16},{9,... | collective-permute-start | bytes 159752 | tf_op jit(solution)/shard_map/ppermute | solution.py:594
  9.3 2.5 %copy.43 = bf16[24,100,512]{2,1,0:T(8,128)(2,1)S(1)} copy(bf16[24,100,512]{2,0,1:T(8,128)(2,1)} %param.18) | data formatting | bytes 4915200 | tf_op args[0]
  14.2 2.5 %collective-permute-start.5 = (bf16[4,16,1664]{2,1,0:T(8,128)(2,1)S(1)}, bf16[4,16,1664]{2,1,0:T(8,128)(2,1)S(1)}, u32[]{:S(2)}, u32[]{:S(2)}) collective-permute-start(bf16[4,16,1664]{2,1,0:T(8,128)(2,1)S(1)} %join.2.refs_2_.refs_1_), channel_id=1, source_target_pairs={{0,6},{1,7},{2,4},{3,5},{4,2},{5,3},{6,0},{7,1},{8,14},{9,15},{10,... | collective-permute-start | bytes 638984 | tf_op jit(solution)/shard_map/ppermute | solution.py:594
  19.4 2.5 %collective-permute-start.12 = (bf16[1,144,512]{2,1,0:T(8,128)(2,1)S(1)}, bf16[1,144,512]{2,1,0:T(8,128)(2,1)S(1)}, u32[]{:S(2)}, u32[]{:S(2)}) collective-permute-start(bf16[1,144,512]{2,1,0:T(8,128)(2,1)S(1)} %pack_hidden.1.refs_1_), channel_id=1, source_target_pairs={{0,24},{1,25},{2,26},{3,27},{4,28},{5,29},{6,30},{7,31},{8,16},{9,... | collective-permute-start | bytes 442376 | tf_op jit(solution)/shard_map/ppermute | solution.py:594
  21.9 3.9 %score_bias.1.refs_5_.refs_3_ = f32[4,104,512]{2,1,0:T(8,128)} custom-call(s32[2]{0:T(128)} %pad_add_fusion.refs_0_, bf16[16,361]{1,0:T(8,128)(2,1)} %refs_1_.4, bf16[4,16,1664]{2,1,0:T(8,128)(2,1)} %copy-done.3), custom_call_target="tpu_custom_call" | custom-call | flops 1000 | bytes 1000 | tf_op jit(solution)/shard_map/score_bias/pallas_call | solution.py:150
  28.4 4.7 %collective-permute-done.11.refs_3_ = bf16[1,144,512]{2,1,0:T(8,128)(2,1)S(1)} collective-permute-done((bf16[1,144,512]{2,1,0:T(8,128)(2,1)S(1)}, bf16[1,144,512]{2,1,0:T(8,128)(2,1)S(1)}, u32[]{:S(2)}, u32[]{:S(2)}) %collective-permute-start.11) | collective-permute-done | bytes 147488 | tf_op jit(solution)/shard_map/ppermute | solution.py:594
  33.0 5.1 %collective-permute-done.10.refs_2_ = bf16[1,144,512]{2,1,0:T(8,128)(2,1)S(1)} collective-permute-done((bf16[1,144,512]{2,1,0:T(8,128)(2,1)S(1)}, bf16[1,144,512]{2,1,0:T(8,128)(2,1)S(1)}, u32[]{:S(2)}, u32[]{:S(2)}) %collective-permute-start.10) | collective-permute-done | bytes 147488 | tf_op jit(solution)/shard_map/ppermute | solution.py:594
  39.7 2.5 %collective-permute-start.15 = (bf16[4,144,512]{2,1,0:T(8,128)(2,1)S(1)}, bf16[4,144,512]{2,1,0:T(8,128)(2,1)}, u32[]{:S(2)}, u32[]{:S(2)}) collective-permute-start(bf16[4,144,512]{2,1,0:T(8,128)(2,1)S(1)} %join.3.refs_12_.refs_1_), channel_id=1, source_target_pairs={{0,6},{1,7},{2,4},{3,5},{4,2},{5,3},{6,0},{7,1},{8,14},{9,15},{10,... | collective-permute-start | bytes 1769480 | tf_op jit(solution)/shard_map/ppermute | solution.py:594
  44.6 15.7 %attn_fwd.1 = (bf16[2496,512]{1,0:T(8,128)(2,1)}, bf16[24,128,1536]{2,1,0:T(8,128)(2,1)}, bf16[24,4,104,512]{3,2,1,0:T(8,128)(2,1)}, bf16[2496,512]{1,0:T(8,128)...) custom-call(s32[2]{0:T(128)} %pad_add_fusion.refs_0_, bf16[24,104,512]{2,1,0:T(8,128)(2,1)} %copy-done, s32[24,100]{1,0:T(8,128)} %refs_2_.5, ...), custom_call_target="tpu_custom_call" | custom-call | flops 19200000000 | bytes 24000000 | tf_op jit(solution)/shard_map/attn_fwd/pallas_call | solution.py:125
  60.4 5.3 %collective-permute-done.14.refs_3_ = bf16[4,144,512]{2,1,0:T(8,128)(2,1)} collective-permute-done((bf16[4,144,512]{2,1,0:T(8,128)(2,1)S(1)}, bf16[4,144,512]{2,1,0:T(8,128)(2,1)}, u32[]{:S(2)}, u32[]{:S(2)}) %collective-permute-start.14) | collective-permute-done | bytes 589856 | tf_op jit(solution)/shard_map/ppermute | solution.py:594
  72.2 32.2 %hidden.1 = (bf16[24,100,512]{2,1,0:T(8,128)(2,1)}, bf16[2496,512]{1,0:T(8,128)(2,1)}, bf16[24,104,512]{2,1,0:T(8,128)(2,1)}, f32[1,2048]{1,0:T(1,128)}, f32[2,5...) custom-call(s32[2]{0:T(128)} %pad_add_fusion.refs_0_, ...), custom_call_target="tpu_custom_call" | custom-call | flops 41600000000 | bytes 52000000 | tf_op jit(solution)/shard_map/hidden/pallas_call | solution.py:125
  104.4 7.1 %collective-permute-start.20 = (bf16[16,144,512]{2,1,0:T(8,128)(2,1)S(1)}, bf16[16,144,512]{2,1,0:T(8,128)(2,1)S(1)}, u32[]{:S(2)}, u32[]{:S(2)}) collective-permute-start(bf16[16,144,512]{2,1,0:T(8,128)(2,1)S(1)} %get-tuple-element.89), channel_id=1, source_target_pairs={{0,1},{1,0},{2,3},{3,2},{4,5},{5,4},{6,7},{7,6},{8,9},{9,8},{10,11... | collective-permute-start | bytes 7077896 | tf_op jit(solution)/shard_map/ppermute | solution.py:594
  111.4 4.2 %collective-permute-done.20.refs_2_ = bf16[16,144,512]{2,1,0:T(8,128)(2,1)S(1)} collective-permute-done((bf16[16,144,512]{2,1,0:T(8,128)(2,1)S(1)}, bf16[16,144,512]{2,1,0:T(8,128)(2,1)S(1)}, u32[]{:S(2)}, u32[]{:S(2)}) %collective-permute-start.20) | collective-permute-done | bytes 2359328 | tf_op jit(solution)/shard_map/ppermute | solution.py:594
  117.5 8.8 %collective-permute-start.21 = (bf16[4,144,512]{2,1,0:T(8,128)(2,1)S(1)}, bf16[4,144,512]{2,1,0:T(8,128)(2,1)S(1)}, u32[]{:S(2)}, u32[]{:S(2)}) collective-permute-start(bf16[4,144,512]{2,1,0:T(8,128)(2,1)S(1)} %get-tuple-element.93), channel_id=1, source_target_pairs={{0,2},{1,3},{2,0},{3,1},{4,6},{5,7},{6,4},{7,5},{8,10},{9,11},{10,... | collective-permute-start | bytes 1769480 | tf_op jit(solution)/shard_map/ppermute | solution.py:594
  127.7 18.9 %attn_back.1 = (bf16[2496,1536]{1,0:T(8,128)(2,1)}, bf16[17,16,1536]{2,1,0:T(8,128)(2,1)S(1)}, bf16[17,16,1536]{2,1,0:T(8,128)(2,1)S(1)}) custom-call(s32[2]{0:T(128)} %pad_add_fusion.refs_0_, bf16[24,128,1536]{2,1,0:T(8,128)(2,1)} %get-tuple-element.82.refs_1_, bf16[24,4,104,512]{3,2,1,0:T(8,128)(2,1)} %get-tuple-element.83.refs_2_, ...), custom_call_target="tpu_custom_call" | custom-call | flops 21600000000 | bytes 27000000 | tf_op jit(solution)/shard_map/attn_back/pallas_call | solution.py:125
  147.5 6.5 %collective-permute-done.22.refs_3_ = bf16[4,144,512]{2,1,0:T(8,128)(2,1)S(1)} collective-permute-done((bf16[4,144,512]{2,1,0:T(8,128)(2,1)S(1)}, bf16[4,144,512]{2,1,0:T(8,128)(2,1)S(1)}, u32[]{:S(2)}, u32[]{:S(2)}) %collective-permute-start.22) | collective-permute-done | bytes 589856 | tf_op jit(solution)/shard_map/ppermute | solution.py:594
  156.3 10.3 %collective-permute-start.28 = (bf16[1,144,512]{2,1,0:T(8,128)(2,1)S(1)}, bf16[1,144,512]{2,1,0:T(8,128)(2,1)S(1)}, u32[]{:S(2)}, u32[]{:S(2)}) collective-permute-start(bf16[1,144,512]{2,1,0:T(8,128)(2,1)S(1)} %get-tuple-element.103), channel_id=1, source_target_pairs={{0,8},{1,9},{2,10},{3,11},{4,12},{5,13},{6,14},{7,15},{8,0},{9,1},... | collective-permute-start | bytes 442376 | tf_op jit(solution)/shard_map/ppermute | solution.py:594
  166.5 3.5 %collective-permute-start.29 = (bf16[1,144,512]{2,1,0:T(8,128)(2,1)S(1)}, bf16[1,144,512]{2,1,0:T(8,128)(2,1)S(1)}, u32[]{:S(2)}, u32[]{:S(2)}) collective-permute-start(bf16[1,144,512]{2,1,0:T(8,128)(2,1)S(1)} %get-tuple-element.104), channel_id=1, source_target_pairs={{0,16},{1,17},{2,18},{3,19},{4,20},{5,21},{6,22},{7,23},{8,24},{9,... | collective-permute-start | bytes 442376 | tf_op jit(solution)/shard_map/ppermute | solution.py:594
  171.5 2.5 %collective-permute-start.25 = (bf16[5,16,1536]{2,1,0:T(8,128)(2,1)S(1)}, bf16[5,16,1536]{2,1,0:T(8,128)(2,1)S(1)}, u32[]{:S(2)}, u32[]{:S(2)}) collective-permute-start(bf16[5,16,1536]{2,1,0:T(8,128)(2,1)S(1)} %get-tuple-element.100), channel_id=1, source_target_pairs={{0,2},{1,3},{2,0},{3,1},{4,6},{5,7},{6,4},{7,5},{8,10},{9,11},{10,... | collective-permute-start | bytes 737288 | tf_op jit(solution)/shard_map/ppermute | solution.py:594
  174.0 5.1 %collective-permute-start.26 = (bf16[5,16,1536]{2,1,0:T(8,128)(2,1)S(1)}, bf16[5,16,1536]{2,1,0:T(8,128)(2,1)S(1)}, u32[]{:S(2)}, u32[]{:S(2)}) collective-permute-start(bf16[5,16,1536]{2,1,0:T(8,128)(2,1)S(1)} %get-tuple-element.101), channel_id=1, source_target_pairs={{0,4},{1,5},{2,6},{3,7},{4,0},{5,1},{6,2},{7,3},{8,12},{9,13},{10,... | collective-permute-start | bytes 737288 | tf_op jit(solution)/shard_map/ppermute | solution.py:594
  179.2 2.3 %collective-permute-start.27 = (bf16[5,16,1536]{2,1,0:T(8,128)(2,1)S(1)}, bf16[5,16,1536]{2,1,0:T(8,128)(2,1)S(1)}, u32[]{:S(2)}, u32[]{:S(2)}) collective-permute-start(bf16[5,16,1536]{2,1,0:T(8,128)(2,1)S(1)} %get-tuple-element.102), channel_id=1, source_target_pairs={{0,6},{1,7},{2,4},{3,5},{4,2},{5,3},{6,0},{7,1},{8,14},{9,15},{10,... | collective-permute-start | bytes 737288 | tf_op jit(solution)/shard_map/ppermute | solution.py:594
  181.5 10.8 %input_grad.1.refs_5_ = bf16[24,100,512]{2,1,0:T(8,128)(2,1)} custom-call(s32[2]{0:T(128)} %pad_add_fusion.refs_0_, bf16[24,104,512]{2,1,0:T(8,128)(2,1)} %copy-done, bf16[24,104,512]{2,1,0:T(8,128)(2,1)} %pad.8.refs_2_, bf16[2496,1536]{1,0:T(8,128)(2,1)} %get-tuple-element.91.refs_3_, bf16[2496,512]{1,0:T(8,128)(2,1)} %get-tuple-element.92.refs_4_, ...), custom_call_target="tpu_custom_call" | custom-call | flops 9600000000 | bytes 12000000 | tf_op jit(solution)/shard_map/input_grad/pallas_call | solution.py:125
  194.8 3.6 %collective-permute-start.32 = (bf16[2,16,1536]{2,1,0:T(8,128)(2,1)S(1)}, bf16[2,16,1536]{2,1,0:T(8,128)(2,1)S(1)}, u32[]{:S(2)}, u32[]{:S(2)}) collective-permute-start(bf16[2,16,1536]{2,1,0:T(8,128)(2,1)S(1)} %get-tuple-element.108), channel_id=1, source_target_pairs={{0,16},{1,17},{2,18},{3,19},{4,20},{5,21},{6,22},{7,23},{8,24},{9,... | collective-permute-start | bytes 294920 | tf_op jit(solution)/shard_map/ppermute | solution.py:594
  206.3 2.5 %finish_joint.1 = (f32[16,1536]{1,0:T(8,128)}, f32[16,361]{1,0:T(8,128)}, f32[1,16]{1,0:T(1,128)}, f32[1,16]{1,0:T(1,128)}, f32[1,16]{1,0:T(1,128)}, /*index=5*/...) custom-call(s32[2]{0:T(128)} %pad_add_fusion.refs_0_, ...), custom_call_target="tpu_custom_call" | custom-call | flops 1000 | bytes 1000 | tf_op jit(solution)/shard_map/finish_joint/pallas_call | solution.py:150
  (133 shorter events, 38.9 us)
Async XLA Ops:
  14.2 11.6 %collective-permute-start.5 = (bf16[4,16,1664]{2,1,0:T(8,128)(2,1)S(1)}, bf16[4,16,1664]{2,1,0:T(8,128)(2,1)S(1)}, u32[]{:S(2)}, u32[]{:S(2)}) collective-permute-start(bf16[4,16,1664]{2,1,0:T(8,128)(2,1)S(1)} %join.2.refs_2_.refs_1_), channel_id=1, source_target_pairs={{0,6},{1,7},{2,4},{3,5},{4,2},{5,3},{6,0},{7,1},{8,14},{9,15},{10,... | collective-permute-start | bytes 638984 | tf_op jit(solution)/shard_map/ppermute | solution.py:594
  16.8 9.2 %collective-permute-start.4 = (bf16[4,16,1664]{2,1,0:T(8,128)(2,1)S(1)}, bf16[4,16,1664]{2,1,0:T(8,128)(2,1)S(1)}, u32[]{:S(2)}, u32[]{:S(2)}) collective-permute-start(bf16[4,16,1664]{2,1,0:T(8,128)(2,1)S(1)} %join.2.refs_2_.refs_1_), channel_id=1, source_target_pairs={{0,4},{1,5},{2,6},{3,7},{4,0},{5,1},{6,2},{7,3},{8,12},{9,13},{10,... | collective-permute-start | bytes 638984 | tf_op jit(solution)/shard_map/ppermute | solution.py:594
  17.3 8.9 %collective-permute-start.3 = (bf16[4,16,1664]{2,1,0:T(8,128)(2,1)S(1)}, bf16[4,16,1664]{2,1,0:T(8,128)(2,1)}, u32[]{:S(2)}, u32[]{:S(2)}) collective-permute-start(bf16[4,16,1664]{2,1,0:T(8,128)(2,1)S(1)} %join.2.refs_2_.refs_1_), channel_id=1, source_target_pairs={{0,2},{1,3},{2,0},{3,1},{4,6},{5,7},{6,4},{7,5},{8,10},{9,11},{10,... | collective-permute-start | bytes 638984 | tf_op jit(solution)/shard_map/ppermute | solution.py:594
  21.9 11.1 %collective-permute-start.11 = (bf16[1,144,512]{2,1,0:T(8,128)(2,1)S(1)}, bf16[1,144,512]{2,1,0:T(8,128)(2,1)S(1)}, u32[]{:S(2)}, u32[]{:S(2)}) collective-permute-start(bf16[1,144,512]{2,1,0:T(8,128)(2,1)S(1)} %pack_hidden.1.refs_1_), channel_id=1, source_target_pairs={{0,16},{1,17},{2,18},{3,19},{4,20},{5,21},{6,22},{7,23},{8,24},{9,... | collective-permute-start | bytes 442376 | tf_op jit(solution)/shard_map/ppermute | solution.py:594
  27.3 14.9 %collective-permute-start.7 = (bf16[4,16,1664]{2,1,0:T(8,128)(2,1)}, bf16[4,16,1664]{2,1,0:T(8,128)(2,1)S(1)}, u32[]{:S(2)}, u32[]{:S(2)}) collective-permute-start(bf16[4,16,1664]{2,1,0:T(8,128)(2,1)} %get-tuple-element.71.refs_5_.refs_7_), channel_id=1, source_target_pairs={{0,1},{1,0},{2,3},{3,2},{4,5},{5,4},{6,7},{7,6},{8,9},{9,8},{10,11... | collective-permute-start | bytes 638984 | tf_op jit(solution)/shard_map/ppermute | solution.py:594
  27.4 15.4 %collective-permute-start.8 = (bf16[4,16,1664]{2,1,0:T(8,128)(2,1)}, bf16[4,16,1664]{2,1,0:T(8,128)(2,1)S(1)}, u32[]{:S(2)}, u32[]{:S(2)}) collective-permute-start(bf16[4,16,1664]{2,1,0:T(8,128)(2,1)} %get-tuple-element.72.refs_6_.refs_8_), channel_id=1, source_target_pairs={{0,1},{1,0},{2,3},{3,2},{4,5},{5,4},{6,7},{7,6},{8,9},{9,8},{10,11... | collective-permute-start | bytes 638984 | tf_op jit(solution)/shard_map/ppermute | solution.py:594
  27.9 15.4 %collective-permute-start.9 = (bf16[4,16,1664]{2,1,0:T(8,128)(2,1)}, bf16[4,16,1664]{2,1,0:T(8,128)(2,1)S(1)}, u32[]{:S(2)}, u32[]{:S(2)}) collective-permute-start(bf16[4,16,1664]{2,1,0:T(8,128)(2,1)} %get-tuple-element.73.refs_7_.refs_9_), channel_id=1, source_target_pairs={{0,1},{1,0},{2,3},{3,2},{4,5},{5,4},{6,7},{7,6},{8,9},{9,8},{10,11... | collective-permute-start | bytes 638984 | tf_op jit(solution)/shard_map/ppermute | solution.py:594
  27.9 15.3 %collective-permute-start.6 = (bf16[4,16,1664]{2,1,0:T(8,128)(2,1)}, bf16[4,16,1664]{2,1,0:T(8,128)(2,1)S(1)}, u32[]{:S(2)}, u32[]{:S(2)}) collective-permute-start(bf16[4,16,1664]{2,1,0:T(8,128)(2,1)} %get-tuple-element.70.refs_5_.refs_4_.refs_6_), channel_id=1, source_target_pairs={{0,1},{1,0},{2,3},{3,2},{4,5},{5,4},{6,7},{7,6},{8,9},{9,8},{10,11... | collective-permute-start | bytes 638984 | tf_op jit(solution)/shard_map/ppermute | solution.py:594
  39.7 20.7 %collective-permute-start.15 = (bf16[4,144,512]{2,1,0:T(8,128)(2,1)S(1)}, bf16[4,144,512]{2,1,0:T(8,128)(2,1)}, u32[]{:S(2)}, u32[]{:S(2)}) collective-permute-start(bf16[4,144,512]{2,1,0:T(8,128)(2,1)S(1)} %join.3.refs_12_.refs_1_), channel_id=1, source_target_pairs={{0,6},{1,7},{2,4},{3,5},{4,2},{5,3},{6,0},{7,1},{8,14},{9,15},{10,... | collective-permute-start | bytes 1769480 | tf_op jit(solution)/shard_map/ppermute | solution.py:594
  42.2 23.5 %collective-permute-start.14 = (bf16[4,144,512]{2,1,0:T(8,128)(2,1)S(1)}, bf16[4,144,512]{2,1,0:T(8,128)(2,1)}, u32[]{:S(2)}, u32[]{:S(2)}) collective-permute-start(bf16[4,144,512]{2,1,0:T(8,128)(2,1)S(1)} %join.3.refs_12_.refs_1_), channel_id=1, source_target_pairs={{0,4},{1,5},{2,6},{3,7},{4,0},{5,1},{6,2},{7,3},{8,12},{9,13},{10,... | collective-permute-start | bytes 1769480 | tf_op jit(solution)/shard_map/ppermute | solution.py:594
  42.7 23.1 %collective-permute-start.13 = (bf16[4,144,512]{2,1,0:T(8,128)(2,1)S(1)}, bf16[4,144,512]{2,1,0:T(8,128)(2,1)}, u32[]{:S(2)}, u32[]{:S(2)}) collective-permute-start(bf16[4,144,512]{2,1,0:T(8,128)(2,1)S(1)} %join.3.refs_12_.refs_1_), channel_id=1, source_target_pairs={{0,2},{1,3},{2,0},{3,1},{4,6},{5,7},{6,4},{7,5},{8,10},{9,11},{10,... | collective-permute-start | bytes 1769480 | tf_op jit(solution)/shard_map/ppermute | solution.py:594
  104.4 11.2 %collective-permute-start.20 = (bf16[16,144,512]{2,1,0:T(8,128)(2,1)S(1)}, bf16[16,144,512]{2,1,0:T(8,128)(2,1)S(1)}, u32[]{:S(2)}, u32[]{:S(2)}) collective-permute-start(bf16[16,144,512]{2,1,0:T(8,128)(2,1)S(1)} %get-tuple-element.89), channel_id=1, source_target_pairs={{0,1},{1,0},{2,3},{3,2},{4,5},{5,4},{6,7},{7,6},{8,9},{9,8},{10,11... | collective-permute-start | bytes 7077896 | tf_op jit(solution)/shard_map/ppermute | solution.py:594
  117.5 30.0 %collective-permute-start.21 = (bf16[4,144,512]{2,1,0:T(8,128)(2,1)S(1)}, bf16[4,144,512]{2,1,0:T(8,128)(2,1)S(1)}, u32[]{:S(2)}, u32[]{:S(2)}) collective-permute-start(bf16[4,144,512]{2,1,0:T(8,128)(2,1)S(1)} %get-tuple-element.93), channel_id=1, source_target_pairs={{0,2},{1,3},{2,0},{3,1},{4,6},{5,7},{6,4},{7,5},{8,10},{9,11},{10,... | collective-permute-start | bytes 1769480 | tf_op jit(solution)/shard_map/ppermute | solution.py:594
  126.3 27.7 %collective-permute-start.22 = (bf16[4,144,512]{2,1,0:T(8,128)(2,1)S(1)}, bf16[4,144,512]{2,1,0:T(8,128)(2,1)S(1)}, u32[]{:S(2)}, u32[]{:S(2)}) collective-permute-start(bf16[4,144,512]{2,1,0:T(8,128)(2,1)S(1)} %get-tuple-element.94), channel_id=1, source_target_pairs={{0,4},{1,5},{2,6},{3,7},{4,0},{5,1},{6,2},{7,3},{8,12},{9,13},{10,... | collective-permute-start | bytes 1769480 | tf_op jit(solution)/shard_map/ppermute | solution.py:594
  126.3 27.7 %collective-permute-start.23 = (bf16[4,144,512]{2,1,0:T(8,128)(2,1)S(1)}, bf16[4,144,512]{2,1,0:T(8,128)(2,1)S(1)}, u32[]{:S(2)}, u32[]{:S(2)}) collective-permute-start(bf16[4,144,512]{2,1,0:T(8,128)(2,1)S(1)} %get-tuple-element.95), channel_id=1, source_target_pairs={{0,6},{1,7},{2,4},{3,5},{4,2},{5,3},{6,0},{7,1},{8,14},{9,15},{10,... | collective-permute-start | bytes 1769480 | tf_op jit(solution)/shard_map/ppermute | solution.py:594
  156.2 13.9 %collective-permute-start.24 = (bf16[17,16,1536]{2,1,0:T(8,128)(2,1)}, bf16[17,16,1536]{2,1,0:T(8,128)(2,1)S(1)}, u32[]{:S(2)}, u32[]{:S(2)}) collective-permute-start(bf16[17,16,1536]{2,1,0:T(8,128)(2,1)} %hand_on.5), channel_id=1, source_target_pairs={{0,1},{1,0},{2,3},{3,2},{4,5},{5,4},{6,7},{7,6},{8,9},{9,8},{10,11... | collective-permute-start | bytes 2506760 | tf_op jit(solution)/shard_map/ppermute | solution.py:594
  156.3 22.9 %collective-permute-start.28 = (bf16[1,144,512]{2,1,0:T(8,128)(2,1)S(1)}, bf16[1,144,512]{2,1,0:T(8,128)(2,1)S(1)}, u32[]{:S(2)}, u32[]{:S(2)}) collective-permute-start(bf16[1,144,512]{2,1,0:T(8,128)(2,1)S(1)} %get-tuple-element.103), channel_id=1, source_target_pairs={{0,8},{1,9},{2,10},{3,11},{4,12},{5,13},{6,14},{7,15},{8,0},{9,1},... | collective-permute-start | bytes 442376 | tf_op jit(solution)/shard_map/ppermute | solution.py:594
  166.5 25.8 %collective-permute-start.29 = (bf16[1,144,512]{2,1,0:T(8,128)(2,1)S(1)}, bf16[1,144,512]{2,1,0:T(8,128)(2,1)S(1)}, u32[]{:S(2)}, u32[]{:S(2)}) collective-permute-start(bf16[1,144,512]{2,1,0:T(8,128)(2,1)S(1)} %get-tuple-element.104), channel_id=1, source_target_pairs={{0,16},{1,17},{2,18},{3,19},{4,20},{5,21},{6,22},{7,23},{8,24},{9,... | collective-permute-start | bytes 442376 | tf_op jit(solution)/shard_map/ppermute | solution.py:594
  170.0 22.2 %collective-permute-start.30 = (bf16[1,144,512]{2,1,0:T(8,128)(2,1)S(1)}, bf16[1,144,512]{2,1,0:T(8,128)(2,1)S(1)}, u32[]{:S(2)}, u32[]{:S(2)}) collective-permute-start(bf16[1,144,512]{2,1,0:T(8,128)(2,1)S(1)} %get-tuple-element.105), channel_id=1, source_target_pairs={{0,24},{1,25},{2,26},{3,27},{4,28},{5,29},{6,30},{7,31},{8,16},{9,... | collective-permute-start | bytes 442376 | tf_op jit(solution)/shard_map/ppermute | solution.py:594
  171.5 20.8 %collective-permute-start.25 = (bf16[5,16,1536]{2,1,0:T(8,128)(2,1)S(1)}, bf16[5,16,1536]{2,1,0:T(8,128)(2,1)S(1)}, u32[]{:S(2)}, u32[]{:S(2)}) collective-permute-start(bf16[5,16,1536]{2,1,0:T(8,128)(2,1)S(1)} %get-tuple-element.100), channel_id=1, source_target_pairs={{0,2},{1,3},{2,0},{3,1},{4,6},{5,7},{6,4},{7,5},{8,10},{9,11},{10,... | collective-permute-start | bytes 737288 | tf_op jit(solution)/shard_map/ppermute | solution.py:594
  174.0 18.3 %collective-permute-start.26 = (bf16[5,16,1536]{2,1,0:T(8,128)(2,1)S(1)}, bf16[5,16,1536]{2,1,0:T(8,128)(2,1)S(1)}, u32[]{:S(2)}, u32[]{:S(2)}) collective-permute-start(bf16[5,16,1536]{2,1,0:T(8,128)(2,1)S(1)} %get-tuple-element.101), channel_id=1, source_target_pairs={{0,4},{1,5},{2,6},{3,7},{4,0},{5,1},{6,2},{7,3},{8,12},{9,13},{10,... | collective-permute-start | bytes 737288 | tf_op jit(solution)/shard_map/ppermute | solution.py:594
  179.2 13.1 %collective-permute-start.27 = (bf16[5,16,1536]{2,1,0:T(8,128)(2,1)S(1)}, bf16[5,16,1536]{2,1,0:T(8,128)(2,1)S(1)}, u32[]{:S(2)}, u32[]{:S(2)}) collective-permute-start(bf16[5,16,1536]{2,1,0:T(8,128)(2,1)S(1)} %get-tuple-element.102), channel_id=1, source_target_pairs={{0,6},{1,7},{2,4},{3,5},{4,2},{5,3},{6,0},{7,1},{8,14},{9,15},{10,... | collective-permute-start | bytes 737288 | tf_op jit(solution)/shard_map/ppermute | solution.py:594
  194.7 10.3 %collective-permute-start.31 = (bf16[2,16,1536]{2,1,0:T(8,128)(2,1)S(1)}, bf16[2,16,1536]{2,1,0:T(8,128)(2,1)S(1)}, u32[]{:S(2)}, u32[]{:S(2)}) collective-permute-start(bf16[2,16,1536]{2,1,0:T(8,128)(2,1)S(1)} %get-tuple-element.107), channel_id=1, source_target_pairs={{0,8},{1,9},{2,10},{3,11},{4,12},{5,13},{6,14},{7,15},{8,0},{9,1},... | collective-permute-start | bytes 294920 | tf_op jit(solution)/shard_map/ppermute | solution.py:594
  194.8 11.4 %collective-permute-start.32 = (bf16[2,16,1536]{2,1,0:T(8,128)(2,1)S(1)}, bf16[2,16,1536]{2,1,0:T(8,128)(2,1)S(1)}, u32[]{:S(2)}, u32[]{:S(2)}) collective-permute-start(bf16[2,16,1536]{2,1,0:T(8,128)(2,1)S(1)} %get-tuple-element.108), channel_id=1, source_target_pairs={{0,16},{1,17},{2,18},{3,19},{4,20},{5,21},{6,22},{7,23},{8,24},{9,... | collective-permute-start | bytes 294920 | tf_op jit(solution)/shard_map/ppermute | solution.py:594
  (42 other events, 295.5 us)

commit v3 on v2

--- a/solution.py
+++ b/solution.py
@@ -401,23 +401,25 @@
     return hi, mid, (rest - mid.astype(F32)).astype(BF)
 
 
-def table_row(scores):
+def table_rows(scores):
     side = 2 * WS - 1
     reach = side * (WS - 1) + WS - 1
     j = lax.broadcasted_iota(jnp.int32, (SEG, 256), 0)
     k = lax.broadcasted_iota(jnp.int32, (SEG, 256), 1)
     pick = jnp.where(k == reach - (side * (j // WS) + j % WS), 1.0, 0.0).astype(BF)
-    u = sum(dot(t, pick) for t in three_terms(scores))
-    u = jnp.concatenate([u, jnp.zeros((TP, 128), F32)], axis=1)
-    u = pltpu.roll(u, 0, 1, stride=1, stride_axis=0)
     r = lax.broadcasted_iota(jnp.int32, (16, TP), 0)
     i = lax.broadcasted_iota(jnp.int32, (16, TP), 1)
     group = jnp.where(r == i // WS, 1.0, 0.0).astype(BF)
-    v = sum(dot(group, t) for t in three_terms(u))
+    rest = jnp.zeros((TP, 128), F32)
     skip = side - WS
-    low = pltpu.roll(v[0:8], 0, 1, stride=skip, stride_axis=0)
-    high = pltpu.roll(v[8:16], 0, 1, stride=skip, stride_axis=0)
-    return jnp.sum(low + pltpu.roll(high, 8 * skip, 1), axis=0, keepdims=True)
+    us = [sum(dot(t, pick) for t in three_terms(v)) for v in scores]
+    us = [jnp.concatenate([u, rest], axis=1) for u in us]
+    us = [pltpu.roll(u, 0, 1, stride=1, stride_axis=0) for u in us]
+    vs = [sum(dot(group, t) for t in three_terms(u)) for u in us]
+    low = [pltpu.roll(v[0:8], 0, 1, stride=skip, stride_axis=0) for v in vs]
+    high = [pltpu.roll(v[8:16], 0, 1, stride=skip, stride_axis=0) for v in vs]
+    high = [pltpu.roll(h, 8 * skip, 1) for h in high]
+    return [jnp.sum(p + q, axis=0, keepdims=True) for p, q in zip(low, high)]
 
 
 def attention_back_body(
@@ -502,9 +504,11 @@
     @pl.when(i == pl.num_programs(0) - 1)
     def _():
         split_blocks(scal[1] & 1, keep_ref, send_ref, 0, BLK, pj)
-        for h in range(width // 32):
-            lanes = slice(SEG * (h % 4), SEG * (h % 4 + 1))
-            small[h : h + 1, 0:384] = table_row(ra[h // 4, :, lanes])
+        for h in range(0, width // 32, 8):
+            heads = range(h, h + 8)
+            lanes = [slice(SEG * (k % 4), SEG * (k % 4 + 1)) for k in heads]
+            rows = table_rows([ra[k // 4, :, c] for k, c in zip(heads, lanes)])
+            small[h : h + 8, 0:384] = jnp.concatenate(rows, axis=0)
         small[0:1, 384:1408] = eb_ref[:, 0:1024]
         small[1:2, 384:1408] = eb_ref[:, 1024:2048]
         small[2:3, 384:896] = sb_ref[0:1, :]

time: 210 us -> 209 us (level)
  transfers between devices with their start and end apart: 34 -> 34, of which waited for: 12 -> 13; matrix products, arithmetic and copies ran while one was open for 5% -> 5% of each run, Pallas kernels for 26% -> 26%
where the time goes in v3:
time: 209 us
  Pallas kernels  94.2 us (45%)
  starting transfers between devices  63.4 us (30%)
  waiting for transfers between devices  30.4 us (15%)
  local copies, waits for them, and re-layouts  18.1 us (9%)
    pallas_call x4, Pallas kernels, call(): pl.pallas_call(without_gate, grid_spec=pltpu.PrefetchScalarGridSpec(num_s...  76.9 us
    ppermute x34, starting transfers between devices, exchange(): return lax.ppermute(v, AXES, [(i, i ^ mask) for i in range(n)])  63.4 us
    ppermute x34, waiting for transfers between devices, exchange(): return lax.ppermute(v, AXES, [(i, i ^ mask) for i in range(n)])  30.4 us
    unnamed x68, local copies, waits for them, and re-layouts  16.3 us
    pallas_call x11, Pallas kernels, small_call(): pl.pallas_call(without_gate, grid_spec=pltpu.PrefetchScalarGridSpec(num_s...  15.3 us
  transfers between devices with their start and end apart: 34, of which 13 were waited for; matrix products, arithmetic and copies ran while one was open for 5% of the time, Pallas kernels for 26%

profile of v3, /device:TPU:0, one launch (start us, length us, event | category | flops | bytes accessed | tf_op | source)
XLA Modules:
  0.0 208.6 jit_solution(15351537022465915151)
XLA Ops:
  3.5 5.1 %collective-permute-start.2 = (bf16[1,16,1664]{2,1,0:T(8,128)(2,1)S(1)}, bf16[1,16,1664]{2,1,0:T(8,128)(2,1)S(1)}, u32[]{:S(2)}, u32[]{:S(2)}) collective-permute-start(bf16[1,16,1664]{2,1,0:T(8,128)(2,1)S(1)} %pack_joint.1.refs_1_.refs_4_.refs_8_), channel_id=1, source_target_pairs={{0,24},{1,25},{2,26},{3,27},{4,28},{5,29},{6,30},{7,31},{8,16},{9,... | collective-permute-start | bytes 159752 | tf_op jit(solution)/shard_map/ppermute | solution.py:598
  9.3 2.5 %copy.43 = bf16[24,100,512]{2,1,0:T(8,128)(2,1)S(1)} copy(bf16[24,100,512]{2,0,1:T(8,128)(2,1)} %param.18) | data formatting | bytes 4915200 | tf_op args[0]
  14.2 2.5 %collective-permute-start.5 = (bf16[4,16,1664]{2,1,0:T(8,128)(2,1)S(1)}, bf16[4,16,1664]{2,1,0:T(8,128)(2,1)S(1)}, u32[]{:S(2)}, u32[]{:S(2)}) collective-permute-start(bf16[4,16,1664]{2,1,0:T(8,128)(2,1)S(1)} %join.2.refs_2_.refs_1_), channel_id=1, source_target_pairs={{0,6},{1,7},{2,4},{3,5},{4,2},{5,3},{6,0},{7,1},{8,14},{9,15},{10,... | collective-permute-start | bytes 638984 | tf_op jit(solution)/shard_map/ppermute | solution.py:598
  19.4 2.5 %collective-permute-start.12 = (bf16[1,144,512]{2,1,0:T(8,128)(2,1)S(1)}, bf16[1,144,512]{2,1,0:T(8,128)(2,1)S(1)}, u32[]{:S(2)}, u32[]{:S(2)}) collective-permute-start(bf16[1,144,512]{2,1,0:T(8,128)(2,1)S(1)} %pack_hidden.1.refs_1_), channel_id=1, source_target_pairs={{0,24},{1,25},{2,26},{3,27},{4,28},{5,29},{6,30},{7,31},{8,16},{9,... | collective-permute-start | bytes 442376 | tf_op jit(solution)/shard_map/ppermute | solution.py:598
  21.9 3.9 %score_bias.1.refs_5_.refs_3_ = f32[4,104,512]{2,1,0:T(8,128)} custom-call(s32[2]{0:T(128)} %pad_add_fusion.refs_0_, bf16[16,361]{1,0:T(8,128)(2,1)} %refs_1_.4, bf16[4,16,1664]{2,1,0:T(8,128)(2,1)} %copy-done.3), custom_call_target="tpu_custom_call" | custom-call | flops 1000 | bytes 1000 | tf_op jit(solution)/shard_map/score_bias/pallas_call | solution.py:150
  28.4 4.7 %collective-permute-done.11.refs_3_ = bf16[1,144,512]{2,1,0:T(8,128)(2,1)S(1)} collective-permute-done((bf16[1,144,512]{2,1,0:T(8,128)(2,1)S(1)}, bf16[1,144,512]{2,1,0:T(8,128)(2,1)S(1)}, u32[]{:S(2)}, u32[]{:S(2)}) %collective-permute-start.11) | collective-permute-done | bytes 147488 | tf_op jit(solution)/shard_map/ppermute | solution.py:598
  33.0 5.1 %collective-permute-done.10.refs_2_ = bf16[1,144,512]{2,1,0:T(8,128)(2,1)S(1)} collective-permute-done((bf16[1,144,512]{2,1,0:T(8,128)(2,1)S(1)}, bf16[1,144,512]{2,1,0:T(8,128)(2,1)S(1)}, u32[]{:S(2)}, u32[]{:S(2)}) %collective-permute-start.10) | collective-permute-done | bytes 147488 | tf_op jit(solution)/shard_map/ppermute | solution.py:598
  39.7 2.5 %collective-permute-start.15 = (bf16[4,144,512]{2,1,0:T(8,128)(2,1)S(1)}, bf16[4,144,512]{2,1,0:T(8,128)(2,1)}, u32[]{:S(2)}, u32[]{:S(2)}) collective-permute-start(bf16[4,144,512]{2,1,0:T(8,128)(2,1)S(1)} %join.3.refs_12_.refs_1_), channel_id=1, source_target_pairs={{0,6},{1,7},{2,4},{3,5},{4,2},{5,3},{6,0},{7,1},{8,14},{9,15},{10,... | collective-permute-start | bytes 1769480 | tf_op jit(solution)/shard_map/ppermute | solution.py:598
  44.6 15.7 %attn_fwd.1 = (bf16[2496,512]{1,0:T(8,128)(2,1)}, bf16[24,128,1536]{2,1,0:T(8,128)(2,1)}, bf16[24,4,104,512]{3,2,1,0:T(8,128)(2,1)}, bf16[2496,512]{1,0:T(8,128)...) custom-call(s32[2]{0:T(128)} %pad_add_fusion.refs_0_, bf16[24,104,512]{2,1,0:T(8,128)(2,1)} %copy-done, s32[24,100]{1,0:T(8,128)} %refs_2_.5, ...), custom_call_target="tpu_custom_call" | custom-call | flops 19200000000 | bytes 24000000 | tf_op jit(solution)/shard_map/attn_fwd/pallas_call | solution.py:125
  60.4 5.3 %collective-permute-done.14.refs_3_ = bf16[4,144,512]{2,1,0:T(8,128)(2,1)} collective-permute-done((bf16[4,144,512]{2,1,0:T(8,128)(2,1)S(1)}, bf16[4,144,512]{2,1,0:T(8,128)(2,1)}, u32[]{:S(2)}, u32[]{:S(2)}) %collective-permute-start.14) | collective-permute-done | bytes 589856 | tf_op jit(solution)/shard_map/ppermute | solution.py:598
  72.2 32.2 %hidden.1 = (bf16[24,100,512]{2,1,0:T(8,128)(2,1)}, bf16[2496,512]{1,0:T(8,128)(2,1)}, bf16[24,104,512]{2,1,0:T(8,128)(2,1)}, f32[1,2048]{1,0:T(1,128)}, f32[2,5...) custom-call(s32[2]{0:T(128)} %pad_add_fusion.refs_0_, ...), custom_call_target="tpu_custom_call" | custom-call | flops 41600000000 | bytes 52000000 | tf_op jit(solution)/shard_map/hidden/pallas_call | solution.py:125
  104.4 7.1 %collective-permute-start.20 = (bf16[16,144,512]{2,1,0:T(8,128)(2,1)S(1)}, bf16[16,144,512]{2,1,0:T(8,128)(2,1)S(1)}, u32[]{:S(2)}, u32[]{:S(2)}) collective-permute-start(bf16[16,144,512]{2,1,0:T(8,128)(2,1)S(1)} %get-tuple-element.89), channel_id=1, source_target_pairs={{0,1},{1,0},{2,3},{3,2},{4,5},{5,4},{6,7},{7,6},{8,9},{9,8},{10,11... | collective-permute-start | bytes 7077896 | tf_op jit(solution)/shard_map/ppermute | solution.py:598
  111.4 4.2 %collective-permute-done.20.refs_2_ = bf16[16,144,512]{2,1,0:T(8,128)(2,1)S(1)} collective-permute-done((bf16[16,144,512]{2,1,0:T(8,128)(2,1)S(1)}, bf16[16,144,512]{2,1,0:T(8,128)(2,1)S(1)}, u32[]{:S(2)}, u32[]{:S(2)}) %collective-permute-start.20) | collective-permute-done | bytes 2359328 | tf_op jit(solution)/shard_map/ppermute | solution.py:598
  117.5 15.0 %collective-permute-start.21 = (bf16[4,144,512]{2,1,0:T(8,128)(2,1)S(1)}, bf16[4,144,512]{2,1,0:T(8,128)(2,1)S(1)}, u32[]{:S(2)}, u32[]{:S(2)}) collective-permute-start(bf16[4,144,512]{2,1,0:T(8,128)(2,1)S(1)} %get-tuple-element.93), channel_id=1, source_target_pairs={{0,2},{1,3},{2,0},{3,1},{4,6},{5,7},{6,4},{7,5},{8,10},{9,11},{10,... | collective-permute-start | bytes 1769480 | tf_op jit(solution)/shard_map/ppermute | solution.py:598
  132.5 4.1 %collective-permute-start.22 = (bf16[4,144,512]{2,1,0:T(8,128)(2,1)S(1)}, bf16[4,144,512]{2,1,0:T(8,128)(2,1)S(1)}, u32[]{:S(2)}, u32[]{:S(2)}) collective-permute-start(bf16[4,144,512]{2,1,0:T(8,128)(2,1)S(1)} %get-tuple-element.94), channel_id=1, source_target_pairs={{0,4},{1,5},{2,6},{3,7},{4,0},{5,1},{6,2},{7,3},{8,12},{9,13},{10,... | collective-permute-start | bytes 1769480 | tf_op jit(solution)/shard_map/ppermute | solution.py:598
  138.1 18.2 %attn_back.1 = (bf16[2496,1536]{1,0:T(8,128)(2,1)}, bf16[17,16,1536]{2,1,0:T(8,128)(2,1)S(1)}, bf16[17,16,1536]{2,1,0:T(8,128)(2,1)S(1)}) custom-call(s32[2]{0:T(128)} %pad_add_fusion.refs_0_, bf16[24,128,1536]{2,1,0:T(8,128)(2,1)} %get-tuple-element.82.refs_1_, bf16[24,4,104,512]{3,2,1,0:T(8,128)(2,1)} %get-tuple-element.83.refs_2_, ...), custom_call_target="tpu_custom_call" | custom-call | flops 21600000000 | bytes 27000000 | tf_op jit(solution)/shard_map/attn_back/pallas_call | solution.py:125
  157.2 5.0 %collective-permute-done.22.refs_3_ = bf16[4,144,512]{2,1,0:T(8,128)(2,1)S(1)} collective-permute-done((bf16[4,144,512]{2,1,0:T(8,128)(2,1)S(1)}, bf16[4,144,512]{2,1,0:T(8,128)(2,1)S(1)}, u32[]{:S(2)}, u32[]{:S(2)}) %collective-permute-start.22) | collective-permute-done | bytes 589856 | tf_op jit(solution)/shard_map/ppermute | solution.py:598
  166.3 4.8 %collective-permute-start.28 = (bf16[1,144,512]{2,1,0:T(8,128)(2,1)S(1)}, bf16[1,144,512]{2,1,0:T(8,128)(2,1)S(1)}, u32[]{:S(2)}, u32[]{:S(2)}) collective-permute-start(bf16[1,144,512]{2,1,0:T(8,128)(2,1)S(1)} %get-tuple-element.103), channel_id=1, source_target_pairs={{0,8},{1,9},{2,10},{3,11},{4,12},{5,13},{6,14},{7,15},{8,0},{9,1},... | collective-permute-start | bytes 442376 | tf_op jit(solution)/shard_map/ppermute | solution.py:598
  171.2 3.0 %collective-permute-start.29 = (bf16[1,144,512]{2,1,0:T(8,128)(2,1)S(1)}, bf16[1,144,512]{2,1,0:T(8,128)(2,1)S(1)}, u32[]{:S(2)}, u32[]{:S(2)}) collective-permute-start(bf16[1,144,512]{2,1,0:T(8,128)(2,1)S(1)} %get-tuple-element.104), channel_id=1, source_target_pairs={{0,16},{1,17},{2,18},{3,19},{4,20},{5,21},{6,22},{7,23},{8,24},{9,... | collective-permute-start | bytes 442376 | tf_op jit(solution)/shard_map/ppermute | solution.py:598
  179.9 10.8 %input_grad.1.refs_5_ = bf16[24,100,512]{2,1,0:T(8,128)(2,1)} custom-call(s32[2]{0:T(128)} %pad_add_fusion.refs_0_, bf16[24,104,512]{2,1,0:T(8,128)(2,1)} %copy-done, bf16[24,104,512]{2,1,0:T(8,128)(2,1)} %pad.8.refs_2_, bf16[2496,1536]{1,0:T(8,128)(2,1)} %get-tuple-element.91.refs_3_, bf16[2496,512]{1,0:T(8,128)(2,1)} %get-tuple-element.92.refs_4_, ...), custom_call_target="tpu_custom_call" | custom-call | flops 9600000000 | bytes 12000000 | tf_op jit(solution)/shard_map/input_grad/pallas_call | solution.py:125
  195.4 3.8 %collective-permute-start.32 = (bf16[2,16,1536]{2,1,0:T(8,128)(2,1)S(1)}, bf16[2,16,1536]{2,1,0:T(8,128)(2,1)S(1)}, u32[]{:S(2)}, u32[]{:S(2)}) collective-permute-start(bf16[2,16,1536]{2,1,0:T(8,128)(2,1)S(1)} %get-tuple-element.108), channel_id=1, source_target_pairs={{0,16},{1,17},{2,18},{3,19},{4,20},{5,21},{6,22},{7,23},{8,24},{9,... | collective-permute-start | bytes 294920 | tf_op jit(solution)/shard_map/ppermute | solution.py:598
  199.2 2.3 %copy.45 = bf16[24,100,512]{2,0,1:T(8,128)(2,1)} copy(bf16[24,100,512]{2,1,0:T(8,128)(2,1)S(1)} %copy-done.20) | data formatting | bytes 4915200
  201.5 2.3 %copy.46 = bf16[24,100,512]{2,0,1:T(8,128)(2,1)} copy(bf16[24,100,512]{2,1,0:T(8,128)(2,1)S(1)} %copy-done.2) | data formatting | bytes 4915200
  205.9 2.5 %finish_joint.1 = (f32[16,1536]{1,0:T(8,128)}, f32[16,361]{1,0:T(8,128)}, f32[1,16]{1,0:T(1,128)}, f32[1,16]{1,0:T(1,128)}, f32[1,16]{1,0:T(1,128)}, /*index=5*/...) custom-call(s32[2]{0:T(128)} %pad_add_fusion.refs_0_, ...), custom_call_target="tpu_custom_call" | custom-call | flops 1000 | bytes 1000 | tf_op jit(solution)/shard_map/finish_joint/pallas_call | solution.py:150
  (133 shorter events, 41.6 us)
Async XLA Ops:
  14.2 11.6 %collective-permute-start.5 = (bf16[4,16,1664]{2,1,0:T(8,128)(2,1)S(1)}, bf16[4,16,1664]{2,1,0:T(8,128)(2,1)S(1)}, u32[]{:S(2)}, u32[]{:S(2)}) collective-permute-start(bf16[4,16,1664]{2,1,0:T(8,128)(2,1)S(1)} %join.2.refs_2_.refs_1_), channel_id=1, source_target_pairs={{0,6},{1,7},{2,4},{3,5},{4,2},{5,3},{6,0},{7,1},{8,14},{9,15},{10,... | collective-permute-start | bytes 638984 | tf_op jit(solution)/shard_map/ppermute | solution.py:598
  16.8 9.2 %collective-permute-start.4 = (bf16[4,16,1664]{2,1,0:T(8,128)(2,1)S(1)}, bf16[4,16,1664]{2,1,0:T(8,128)(2,1)S(1)}, u32[]{:S(2)}, u32[]{:S(2)}) collective-permute-start(bf16[4,16,1664]{2,1,0:T(8,128)(2,1)S(1)} %join.2.refs_2_.refs_1_), channel_id=1, source_target_pairs={{0,4},{1,5},{2,6},{3,7},{4,0},{5,1},{6,2},{7,3},{8,12},{9,13},{10,... | collective-permute-start | bytes 638984 | tf_op jit(solution)/shard_map/ppermute | solution.py:598
  17.3 8.9 %collective-permute-start.3 = (bf16[4,16,1664]{2,1,0:T(8,128)(2,1)S(1)}, bf16[4,16,1664]{2,1,0:T(8,128)(2,1)}, u32[]{:S(2)}, u32[]{:S(2)}) collective-permute-start(bf16[4,16,1664]{2,1,0:T(8,128)(2,1)S(1)} %join.2.refs_2_.refs_1_), channel_id=1, source_target_pairs={{0,2},{1,3},{2,0},{3,1},{4,6},{5,7},{6,4},{7,5},{8,10},{9,11},{10,... | collective-permute-start | bytes 638984 | tf_op jit(solution)/shard_map/ppermute | solution.py:598
  19.4 8.6 %collective-permute-start.12 = (bf16[1,144,512]{2,1,0:T(8,128)(2,1)S(1)}, bf16[1,144,512]{2,1,0:T(8,128)(2,1)S(1)}, u32[]{:S(2)}, u32[]{:S(2)}) collective-permute-start(bf16[1,144,512]{2,1,0:T(8,128)(2,1)S(1)} %pack_hidden.1.refs_1_), channel_id=1, source_target_pairs={{0,24},{1,25},{2,26},{3,27},{4,28},{5,29},{6,30},{7,31},{8,16},{9,... | collective-permute-start | bytes 442376 | tf_op jit(solution)/shard_map/ppermute | solution.py:598
  21.9 11.1 %collective-permute-start.11 = (bf16[1,144,512]{2,1,0:T(8,128)(2,1)S(1)}, bf16[1,144,512]{2,1,0:T(8,128)(2,1)S(1)}, u32[]{:S(2)}, u32[]{:S(2)}) collective-permute-start(bf16[1,144,512]{2,1,0:T(8,128)(2,1)S(1)} %pack_hidden.1.refs_1_), channel_id=1, source_target_pairs={{0,16},{1,17},{2,18},{3,19},{4,20},{5,21},{6,22},{7,23},{8,24},{9,... | collective-permute-start | bytes 442376 | tf_op jit(solution)/shard_map/ppermute | solution.py:598
  27.3 14.9 %collective-permute-start.7 = (bf16[4,16,1664]{2,1,0:T(8,128)(2,1)}, bf16[4,16,1664]{2,1,0:T(8,128)(2,1)S(1)}, u32[]{:S(2)}, u32[]{:S(2)}) collective-permute-start(bf16[4,16,1664]{2,1,0:T(8,128)(2,1)} %get-tuple-element.71.refs_5_.refs_7_), channel_id=1, source_target_pairs={{0,1},{1,0},{2,3},{3,2},{4,5},{5,4},{6,7},{7,6},{8,9},{9,8},{10,11... | collective-permute-start | bytes 638984 | tf_op jit(solution)/shard_map/ppermute | solution.py:598
  27.4 15.4 %collective-permute-start.8 = (bf16[4,16,1664]{2,1,0:T(8,128)(2,1)}, bf16[4,16,1664]{2,1,0:T(8,128)(2,1)S(1)}, u32[]{:S(2)}, u32[]{:S(2)}) collective-permute-start(bf16[4,16,1664]{2,1,0:T(8,128)(2,1)} %get-tuple-element.72.refs_6_.refs_8_), channel_id=1, source_target_pairs={{0,1},{1,0},{2,3},{3,2},{4,5},{5,4},{6,7},{7,6},{8,9},{9,8},{10,11... | collective-permute-start | bytes 638984 | tf_op jit(solution)/shard_map/ppermute | solution.py:598
  27.9 15.4 %collective-permute-start.9 = (bf16[4,16,1664]{2,1,0:T(8,128)(2,1)}, bf16[4,16,1664]{2,1,0:T(8,128)(2,1)S(1)}, u32[]{:S(2)}, u32[]{:S(2)}) collective-permute-start(bf16[4,16,1664]{2,1,0:T(8,128)(2,1)} %get-tuple-element.73.refs_7_.refs_9_), channel_id=1, source_target_pairs={{0,1},{1,0},{2,3},{3,2},{4,5},{5,4},{6,7},{7,6},{8,9},{9,8},{10,11... | collective-permute-start | bytes 638984 | tf_op jit(solution)/shard_map/ppermute | solution.py:598
  27.9 15.3 %collective-permute-start.6 = (bf16[4,16,1664]{2,1,0:T(8,128)(2,1)}, bf16[4,16,1664]{2,1,0:T(8,128)(2,1)S(1)}, u32[]{:S(2)}, u32[]{:S(2)}) collective-permute-start(bf16[4,16,1664]{2,1,0:T(8,128)(2,1)} %get-tuple-element.70.refs_5_.refs_4_.refs_6_), channel_id=1, source_target_pairs={{0,1},{1,0},{2,3},{3,2},{4,5},{5,4},{6,7},{7,6},{8,9},{9,8},{10,11... | collective-permute-start | bytes 638984 | tf_op jit(solution)/shard_map/ppermute | solution.py:598
  39.7 20.7 %collective-permute-start.15 = (bf16[4,144,512]{2,1,0:T(8,128)(2,1)S(1)}, bf16[4,144,512]{2,1,0:T(8,128)(2,1)}, u32[]{:S(2)}, u32[]{:S(2)}) collective-permute-start(bf16[4,144,512]{2,1,0:T(8,128)(2,1)S(1)} %join.3.refs_12_.refs_1_), channel_id=1, source_target_pairs={{0,6},{1,7},{2,4},{3,5},{4,2},{5,3},{6,0},{7,1},{8,14},{9,15},{10,... | collective-permute-start | bytes 1769480 | tf_op jit(solution)/shard_map/ppermute | solution.py:598
  42.2 23.5 %collective-permute-start.14 = (bf16[4,144,512]{2,1,0:T(8,128)(2,1)S(1)}, bf16[4,144,512]{2,1,0:T(8,128)(2,1)}, u32[]{:S(2)}, u32[]{:S(2)}) collective-permute-start(bf16[4,144,512]{2,1,0:T(8,128)(2,1)S(1)} %join.3.refs_12_.refs_1_), channel_id=1, source_target_pairs={{0,4},{1,5},{2,6},{3,7},{4,0},{5,1},{6,2},{7,3},{8,12},{9,13},{10,... | collective-permute-start | bytes 1769480 | tf_op jit(solution)/shard_map/ppermute | solution.py:598
  42.7 23.1 %collective-permute-start.13 = (bf16[4,144,512]{2,1,0:T(8,128)(2,1)S(1)}, bf16[4,144,512]{2,1,0:T(8,128)(2,1)}, u32[]{:S(2)}, u32[]{:S(2)}) collective-permute-start(bf16[4,144,512]{2,1,0:T(8,128)(2,1)S(1)} %join.3.refs_12_.refs_1_), channel_id=1, source_target_pairs={{0,2},{1,3},{2,0},{3,1},{4,6},{5,7},{6,4},{7,5},{8,10},{9,11},{10,... | collective-permute-start | bytes 1769480 | tf_op jit(solution)/shard_map/ppermute | solution.py:598
  104.4 11.2 %collective-permute-start.20 = (bf16[16,144,512]{2,1,0:T(8,128)(2,1)S(1)}, bf16[16,144,512]{2,1,0:T(8,128)(2,1)S(1)}, u32[]{:S(2)}, u32[]{:S(2)}) collective-permute-start(bf16[16,144,512]{2,1,0:T(8,128)(2,1)S(1)} %get-tuple-element.89), channel_id=1, source_target_pairs={{0,1},{1,0},{2,3},{3,2},{4,5},{5,4},{6,7},{7,6},{8,9},{9,8},{10,11... | collective-permute-start | bytes 7077896 | tf_op jit(solution)/shard_map/ppermute | solution.py:598
  117.5 39.7 %collective-permute-start.21 = (bf16[4,144,512]{2,1,0:T(8,128)(2,1)S(1)}, bf16[4,144,512]{2,1,0:T(8,128)(2,1)S(1)}, u32[]{:S(2)}, u32[]{:S(2)}) collective-permute-start(bf16[4,144,512]{2,1,0:T(8,128)(2,1)S(1)} %get-tuple-element.93), channel_id=1, source_target_pairs={{0,2},{1,3},{2,0},{3,1},{4,6},{5,7},{6,4},{7,5},{8,10},{9,11},{10,... | collective-permute-start | bytes 1769480 | tf_op jit(solution)/shard_map/ppermute | solution.py:598
  132.5 29.7 %collective-permute-start.22 = (bf16[4,144,512]{2,1,0:T(8,128)(2,1)S(1)}, bf16[4,144,512]{2,1,0:T(8,128)(2,1)S(1)}, u32[]{:S(2)}, u32[]{:S(2)}) collective-permute-start(bf16[4,144,512]{2,1,0:T(8,128)(2,1)S(1)} %get-tuple-element.94), channel_id=1, source_target_pairs={{0,4},{1,5},{2,6},{3,7},{4,0},{5,1},{6,2},{7,3},{8,12},{9,13},{10,... | collective-permute-start | bytes 1769480 | tf_op jit(solution)/shard_map/ppermute | solution.py:598
  136.6 27.5 %collective-permute-start.23 = (bf16[4,144,512]{2,1,0:T(8,128)(2,1)S(1)}, bf16[4,144,512]{2,1,0:T(8,128)(2,1)S(1)}, u32[]{:S(2)}, u32[]{:S(2)}) collective-permute-start(bf16[4,144,512]{2,1,0:T(8,128)(2,1)S(1)} %get-tuple-element.95), channel_id=1, source_target_pairs={{0,6},{1,7},{2,4},{3,5},{4,2},{5,3},{6,0},{7,1},{8,14},{9,15},{10,... | collective-permute-start | bytes 1769480 | tf_op jit(solution)/shard_map/ppermute | solution.py:598
  166.3 12.1 %collective-permute-start.28 = (bf16[1,144,512]{2,1,0:T(8,128)(2,1)S(1)}, bf16[1,144,512]{2,1,0:T(8,128)(2,1)S(1)}, u32[]{:S(2)}, u32[]{:S(2)}) collective-permute-start(bf16[1,144,512]{2,1,0:T(8,128)(2,1)S(1)} %get-tuple-element.103), channel_id=1, source_target_pairs={{0,8},{1,9},{2,10},{3,11},{4,12},{5,13},{6,14},{7,15},{8,0},{9,1},... | collective-permute-start | bytes 442376 | tf_op jit(solution)/shard_map/ppermute | solution.py:598
  171.2 19.5 %collective-permute-start.29 = (bf16[1,144,512]{2,1,0:T(8,128)(2,1)S(1)}, bf16[1,144,512]{2,1,0:T(8,128)(2,1)S(1)}, u32[]{:S(2)}, u32[]{:S(2)}) collective-permute-start(bf16[1,144,512]{2,1,0:T(8,128)(2,1)S(1)} %get-tuple-element.104), channel_id=1, source_target_pairs={{0,16},{1,17},{2,18},{3,19},{4,20},{5,21},{6,22},{7,23},{8,24},{9,... | collective-permute-start | bytes 442376 | tf_op jit(solution)/shard_map/ppermute | solution.py:598
  174.1 16.5 %collective-permute-start.30 = (bf16[1,144,512]{2,1,0:T(8,128)(2,1)S(1)}, bf16[1,144,512]{2,1,0:T(8,128)(2,1)S(1)}, u32[]{:S(2)}, u32[]{:S(2)}) collective-permute-start(bf16[1,144,512]{2,1,0:T(8,128)(2,1)S(1)} %get-tuple-element.105), channel_id=1, source_target_pairs={{0,24},{1,25},{2,26},{3,27},{4,28},{5,29},{6,30},{7,31},{8,16},{9,... | collective-permute-start | bytes 442376 | tf_op jit(solution)/shard_map/ppermute | solution.py:598
  175.6 15.1 %collective-permute-start.25 = (bf16[5,16,1536]{2,1,0:T(8,128)(2,1)S(1)}, bf16[5,16,1536]{2,1,0:T(8,128)(2,1)S(1)}, u32[]{:S(2)}, u32[]{:S(2)}) collective-permute-start(bf16[5,16,1536]{2,1,0:T(8,128)(2,1)S(1)} %get-tuple-element.100), channel_id=1, source_target_pairs={{0,2},{1,3},{2,0},{3,1},{4,6},{5,7},{6,4},{7,5},{8,10},{9,11},{10,... | collective-permute-start | bytes 737288 | tf_op jit(solution)/shard_map/ppermute | solution.py:598
  176.5 14.2 %collective-permute-start.26 = (bf16[5,16,1536]{2,1,0:T(8,128)(2,1)S(1)}, bf16[5,16,1536]{2,1,0:T(8,128)(2,1)S(1)}, u32[]{:S(2)}, u32[]{:S(2)}) collective-permute-start(bf16[5,16,1536]{2,1,0:T(8,128)(2,1)S(1)} %get-tuple-element.101), channel_id=1, source_target_pairs={{0,4},{1,5},{2,6},{3,7},{4,0},{5,1},{6,2},{7,3},{8,12},{9,13},{10,... | collective-permute-start | bytes 737288 | tf_op jit(solution)/shard_map/ppermute | solution.py:598
  178.4 12.3 %collective-permute-start.27 = (bf16[5,16,1536]{2,1,0:T(8,128)(2,1)S(1)}, bf16[5,16,1536]{2,1,0:T(8,128)(2,1)S(1)}, u32[]{:S(2)}, u32[]{:S(2)}) collective-permute-start(bf16[5,16,1536]{2,1,0:T(8,128)(2,1)S(1)} %get-tuple-element.102), channel_id=1, source_target_pairs={{0,6},{1,7},{2,4},{3,5},{4,2},{5,3},{6,0},{7,1},{8,14},{9,15},{10,... | collective-permute-start | bytes 737288 | tf_op jit(solution)/shard_map/ppermute | solution.py:598
  193.1 11.9 %collective-permute-start.31 = (bf16[2,16,1536]{2,1,0:T(8,128)(2,1)S(1)}, bf16[2,16,1536]{2,1,0:T(8,128)(2,1)S(1)}, u32[]{:S(2)}, u32[]{:S(2)}) collective-permute-start(bf16[2,16,1536]{2,1,0:T(8,128)(2,1)S(1)} %get-tuple-element.107), channel_id=1, source_target_pairs={{0,8},{1,9},{2,10},{3,11},{4,12},{5,13},{6,14},{7,15},{8,0},{9,1},... | collective-permute-start | bytes 294920 | tf_op jit(solution)/shard_map/ppermute | solution.py:598
  195.4 10.5 %collective-permute-start.32 = (bf16[2,16,1536]{2,1,0:T(8,128)(2,1)S(1)}, bf16[2,16,1536]{2,1,0:T(8,128)(2,1)S(1)}, u32[]{:S(2)}, u32[]{:S(2)}) collective-permute-start(bf16[2,16,1536]{2,1,0:T(8,128)(2,1)S(1)} %get-tuple-element.108), channel_id=1, source_target_pairs={{0,16},{1,17},{2,18},{3,19},{4,20},{5,21},{6,22},{7,23},{8,24},{9,... | collective-permute-start | bytes 294920 | tf_op jit(solution)/shard_map/ppermute | solution.py:598
  (42 other events, 290.8 us)
